TPU v7x, 256 devices: a whole 4x4x8 slice. The times are simulated.
256 devices in a mesh: exp: 16 (over z, core), trow: 4 (over y), tcol: 4 (over x).
Axes of the slice: x: 4, y: 4, z: 8, core: 2. Of those that a mesh axis runs over, the one named last changes fastest.
Arguments:
- stamps: bfloat16 [32, 1536, 1536], P('exp', 'trow', 'tcol'), may hold values from -6 to 6
- footprint: int32 [32, 4], P('exp'), may hold values from 0 to 4, as said below
- psf_anchor: int32 [32, 2], P('exp'), may hold values from 0 to 1535
- psf_degree: int32 [32], P('exp'), may hold values from 1 to 3
- psf_powers: int32 [32, 10, 2], P('exp'), may hold values from 0 to 3, as said below
- psf_basis: float32 [32, 10, 1024], P('exp'), may hold values from -0.1875 to 0.1875
- flux: float32 [32], P('exp'), may hold values from 0.1 to 0.4
- variance: float32 [32], P('exp'), may hold values from 0.5 to 2
Outputs:
- coadd: float32 [4, 384, 1536], P('trow', 'exp', 'tcol')
Inputs may be any that keep to these rules, and one draw needn't show every extreme that they name: `footprint`: each row is a rectangle of tiles with row_lo < row_hi and col_lo < col_hi; for each g, exposures 2g and 2g + 1 (the two held by one device along `exp`) both cover at least one common tile. `psf_powers`: each exposure's rows are the ten pairs (p, q) with p + q <= 3, each once.
All inputs are finite; a program needn't handle non-finite values.
Results may differ from a plain program's by a relative error of at most 0.0068.
Values may be sent and summed in bfloat16 or wider, within the bound.
A program may use at most 192 MiB of HBM per device.

v0:
```python
import math

import jax
import jax.numpy as jnp
from jax import lax
from jax.sharding import PartitionSpec as P

TILE = 512
HALO = 64
PS = 32
CORE = 384


def padded(block, sides, width):
    for axis, dim in sides:
        count = lax.axis_size(axis)
        forward = [(i, i + 1) for i in range(count - 1)]
        backward = [(target, source) for source, target in forward]
        low = lax.ppermute(
            lax.slice_in_dim(block, block.shape[dim] - width, None, axis=dim), axis, forward
        )
        high = lax.ppermute(lax.slice_in_dim(block, 0, width, axis=dim), axis, backward)
        block = jnp.concatenate([low, block, high], axis=dim)
    return block


def spectral_tables():
    idx = jnp.arange(TILE, dtype=jnp.int32)
    prod = idx[:, None] * idx[None, :] % TILE
    angle = prod.astype(jnp.float32) * (2.0 * math.pi / TILE)
    scale = 1.0 / math.sqrt(TILE)
    cosine = jnp.cos(angle) * scale
    sine = jnp.sin(angle) * scale
    return (cosine.astype(jnp.bfloat16), (-sine).astype(jnp.bfloat16), cosine, sine)


def psf_tables():
    idx = jnp.arange(TILE, dtype=jnp.int32)
    offsets = jnp.arange(PS, dtype=jnp.int32) - PS // 2
    prod = idx[:, None] * offsets[None, :] % TILE
    angle = prod.astype(jnp.float32) * (2.0 * math.pi / TILE)
    return (jnp.cos(angle).astype(jnp.bfloat16), (-jnp.sin(angle)).astype(jnp.bfloat16))


def taper_plane():
    idx = jnp.arange(TILE, dtype=jnp.int32)
    dist = jnp.minimum(idx, TILE - 1 - idx).astype(jnp.float32)
    ramp = jnp.sin(0.5 * math.pi * (dist + 0.5) / HALO) ** 2
    line = jnp.where(dist >= HALO, jnp.float32(1.0), ramp)
    return line[:, None] * line[None, :]


def monomial(value, power):
    return jnp.where(
        power == 0,
        1.0,
        jnp.where(power == 1, value, jnp.where(power == 2, value * value, value * value * value)),
    )


def render(basis, powers, degree, anchor, row_tile, col_tile, sky_half):
    ux = (col_tile * CORE + CORE // 2 - anchor[..., 1]).astype(jnp.float32) / sky_half
    uy = (row_tile * CORE + CORE // 2 - anchor[..., 0]).astype(jnp.float32) / sky_half
    px = powers[..., 0]
    qy = powers[..., 1]
    keep = (px + qy <= degree[..., None]).astype(jnp.float32)
    term = monomial(ux[..., None], px) * monomial(uy[..., None], qy) * keep
    return jnp.sum(term[..., None] * basis, axis=-2).astype(jnp.bfloat16)


def image_spectrum(plane, fwd_re, fwd_im):
    half_re = jnp.dot(fwd_re, plane, preferred_element_type=jnp.float32).astype(jnp.bfloat16)
    half_im = jnp.dot(fwd_im, plane, preferred_element_type=jnp.float32).astype(jnp.bfloat16)
    spec_re = jnp.dot(half_re, fwd_re.T, preferred_element_type=jnp.float32) - jnp.dot(
        half_im, fwd_im.T, preferred_element_type=jnp.float32
    )
    spec_im = jnp.dot(half_re, fwd_im.T, preferred_element_type=jnp.float32) + jnp.dot(
        half_im, fwd_re.T, preferred_element_type=jnp.float32
    )
    return (spec_re, spec_im)


def psf_spectrum(stamp, pg_re, pg_im):
    lift_re = jnp.dot(pg_re, stamp, preferred_element_type=jnp.float32).astype(jnp.bfloat16)
    lift_im = jnp.dot(pg_im, stamp, preferred_element_type=jnp.float32).astype(jnp.bfloat16)
    otf_re = jnp.dot(lift_re, pg_re.T, preferred_element_type=jnp.float32) - jnp.dot(
        lift_im, pg_im.T, preferred_element_type=jnp.float32
    )
    otf_im = jnp.dot(lift_re, pg_im.T, preferred_element_type=jnp.float32) + jnp.dot(
        lift_im, pg_re.T, preferred_element_type=jnp.float32
    )
    return (otf_re, otf_im)


def body(stamps, footprint, psf_anchor, psf_degree, psf_powers, psf_basis, flux, variance):
    fwd_re, fwd_im, inv_re, inv_im = spectral_tables()
    pg_re, pg_im = psf_tables()
    taper = taper_plane()
    row_tile = lax.axis_index("trow")
    col_tile = lax.axis_index("tcol")
    group = lax.axis_index("exp")
    groups = lax.axis_size("exp")
    sky_half = 0.5 * CORE * lax.axis_size("tcol")
    active = (
        (footprint[:, 0] <= row_tile)
        & (row_tile < footprint[:, 1])
        & (footprint[:, 2] <= col_tile)
        & (col_tile < footprint[:, 3])
    )
    masked = jnp.where(active[:, None, None], stamps, jnp.zeros((), jnp.bfloat16))
    extended = padded(masked, (("trow", 1), ("tcol", 2)), HALO)
    apodized = (extended.astype(jnp.float32) * taper).astype(jnp.bfloat16)
    rendered = render(psf_basis, psf_powers, psf_degree, psf_anchor, row_tile, col_tile, sky_half)
    weight_num = jnp.where(active, flux / variance, 0.0)
    weight_den = jnp.where(active, flux * flux / variance, 0.0)
    zero_plane = jnp.zeros((TILE, TILE), jnp.float32)
    high = lax.Precision.HIGHEST
    core_re = inv_re[:, HALO : HALO + CORE]
    core_im = inv_im[:, HALO : HALO + CORE]
    out_rows = CORE // groups
    order = jnp.argsort(jnp.where(active, 0, 1).astype(jnp.int32), stable=True)
    count = jnp.sum(active.astype(jnp.int32))

    def own_step(step, carry):
        j = order[step]
        plane = lax.dynamic_index_in_dim(apodized, j, 0, keepdims=False)
        spec_re, spec_im = image_spectrum(plane, fwd_re, fwd_im)
        stamp = lax.dynamic_index_in_dim(rendered, j, 0, keepdims=False).reshape(PS, PS)
        otf_re, otf_im = psf_spectrum(stamp, pg_re, pg_im)
        wnum = weight_num[j]
        wden = weight_den[j]
        return (
            carry[0] + wnum * (otf_re * spec_re + otf_im * spec_im),
            carry[1] + wnum * (otf_re * spec_im - otf_im * spec_re),
            carry[2] + wden * (otf_re * otf_re + otf_im * otf_im),
        )

    num_re, num_im, den = lax.fori_loop(0, count, own_step, (zero_plane, zero_plane, zero_plane))
    sum_re, sum_im, sum_den = lax.psum((num_re, num_im, den), "exp")
    norm = jnp.sqrt(sum_den + 1.0)
    spec_re = sum_re / norm
    spec_im = sum_im / norm
    temp_re = jnp.dot(spec_re, core_re, precision=high) - jnp.dot(spec_im, core_im, precision=high)
    temp_im = jnp.dot(spec_re, core_im, precision=high) + jnp.dot(spec_im, core_re, precision=high)
    left_re = lax.dynamic_slice(inv_re, (HALO + group * out_rows, 0), (out_rows, TILE))
    left_im = lax.dynamic_slice(inv_im, (HALO + group * out_rows, 0), (out_rows, TILE))
    image = jnp.dot(left_re, temp_re, precision=high) - jnp.dot(left_im, temp_im, precision=high)
    return image.reshape(1, out_rows, CORE)


def solution(mesh):
    in_specs = (
        P("exp", "trow", "tcol"),
        P("exp", None),
        P("exp", None),
        P("exp"),
        P("exp", None, None),
        P("exp", None, None),
        P("exp"),
        P("exp"),
    )
    out_specs = P("trow", "exp", "tcol")
    return jax.shard_map(body, mesh=mesh, in_specs=in_specs, out_specs=out_specs, check_vma=False)
```

profile of v0, /device:TPU:1, one launch (start us, length us, event | category | flops | bytes accessed | tf_op | source)
XLA Modules:
  0.0 277.6 jit_solution(3840842352247347579)
XLA Ops:
  6.5 0.0 all-reduce.3.cloned.1.call-start
  6.5 1.0 and_reduce_fusion
  7.6 0.0 copy-start.10
  7.6 0.0 copy-start.7
  7.6 0.0 copy-start.8
  7.6 0.0 copy-start.11
  7.6 1.2 broadcast_select_fusion
  8.9 4.0 %collective-permute-start = (bf16[2,64,384]{2,1,0:T(8,128)(2,1)S(1)}, bf16[2,64,384]{2,1,0:T(8,128)(2,1)S(1)}, u32[]{:S(2)}, u32[]{:S(2)}) collective-permute-start(bf16[2,64,384]{2,1,0:T(8,128)(2,1)S(1)} %get-tuple-element.253), channel_id=1, source_target_pairs={{0,4},{4,8},{8,12},{1,5},{5,9},{9,13},{2,6},{6,10},{10,14},{3,7},{... | collective-permute-start | bytes 294920 | tf_op jit(solution)/shard_map/ppermute | solution.py:19
  12.9 1.3 collective-permute-start.1
  14.3 0.0 copy-start.6
  14.3 0.1 broadcast_multiply_fusion
  14.4 0.0 copy-done.9
  14.4 0.0 copy-done.10
  14.4 0.0 copy-done.7
  14.5 0.3 multiply_reduce_fusion.2
  14.7 0.0 copy-done.11
  14.7 0.1 compare_select_fusion.6
  14.8 0.6 broadcast_select_fusion.1
  15.4 0.0 collective-permute-done
  15.4 2.8 %collective-permute-done.1 = bf16[2,64,384]{2,1,0:T(8,128)(2,1)S(1)} collective-permute-done((bf16[2,64,384]{2,1,0:T(8,128)(2,1)S(1)}, bf16[2,64,384]{2,1,0:T(8,128)(2,1)S(1)}, u32[]{:S(2)}, u32[]{:S(2)}) %collective-permute-start.1) | collective-permute-done | bytes 98336 | tf_op jit(solution)/shard_map/ppermute | solution.py:22
  18.3 0.1 pad_maximum_fusion.2
  18.4 3.1 %collective-permute-start.2 = (bf16[2,512,64]{2,1,0:T(8,128)(2,1)S(1)}, bf16[2,512,64]{2,1,0:T(8,128)(2,1)S(1)}, u32[]{:S(2)}, u32[]{:S(2)}) collective-permute-start(bf16[2,512,64]{2,1,0:T(8,128)(2,1)S(1)} %get-tuple-element.251), channel_id=1, source_target_pairs={{0,1},{1,2},{2,3},{4,5},{5,6},{6,7},{8,9},{9,10},{10,11},{12,13},{... | collective-permute-start | bytes 393224 | tf_op jit(solution)/shard_map/ppermute | solution.py:19
  21.5 1.3 collective-permute-start.3
  22.9 0.1 copy.9
  22.9 0.7 sort.17
  23.6 0.1 multiply_reduce_fusion
  23.7 1.1 collective-permute-done.2
  24.8 3.8 %collective-permute-done.3 = bf16[2,512,64]{2,1,0:T(8,128)(2,1)S(1)} collective-permute-done((bf16[2,512,64]{2,1,0:T(8,128)(2,1)S(1)}, bf16[2,512,64]{2,1,0:T(8,128)(2,1)S(1)}, u32[]{:S(2)}, u32[]{:S(2)}) %collective-permute-start.3) | collective-permute-done | bytes 131104 | tf_op jit(solution)/shard_map/ppermute | solution.py:22
  28.7 1.7 multiply_convert_fusion.4
  30.3 0.1 broadcast_in_dim.100
  30.4 0.1 broadcast_in_dim.100.clone
  30.6 0.1 broadcast_in_dim.100.clone.1
  30.7 55.5 %while.17 = (s32[]{:T(128)}, f32[512,512]{1,0:T(8,128)S(1)}, f32[512,512]{1,0:T(8,128)S(1)}, f32[512,512]{1,0:T(8,128)S(1)}, s32[]{:T(128)}, /*index=5*/s32[2]{0...) while((s32[]{:T(128)}, f32[512,512]{1,0:T(8,128)S(1)}, ...), condition=%wide.region_4.5_spmd.clone.clone.clone, body=%wide.region_3.4_spmd.clone.clone.clone.sunk | while | flops 1712832512 | bytes 37958740 | solution.py:138
  31.3 0.7 dynamic_slice.62
  34.0 5.5 %convolution_convert_fusion.8 = bf16[512,512]{1,0:T(8,128)(2,1)S(1)} fusion(bf16[2,512,512]{2,1,0:T(8,128)(2,1)} %get-tuple-element.369, s32[]{:T(128)S(6)} %select_n.247), kind=kOutput, calls=%fused_computation.12.clone.1 | convolution fusion | flops 272891904 | bytes 1048580 | tf_op jit(solution)/shard_map/while/body/dot_general | solution.py:72
  39.5 5.0 %fusion.156 = f32[512,512]{1,0:T(8,128)S(1)} fusion(bf16[512,512]{1,0:T(8,128)(2,1)S(1)} %convolution_convert_fusion.8), kind=kOutput, calls=%fused_computation.29.clone.1 | convolution fusion | flops 272891904 | bytes 1572864 | tf_op jit(solution)/shard_map/while/body/dot_general | solution.py:77
  44.5 4.4 %convolution_convert_fusion.9 = bf16[512,512]{1,0:T(8,128)(2,1)S(1)} fusion(bf16[2,512,512]{2,1,0:T(8,128)(2,1)S(1)} %copy-done.5, s32[]{:T(128)S(6)} %select_n.247), kind=kOutput, calls=%fused_computation.11.clone.1 | convolution fusion | flops 273154048 | bytes 1048580 | tf_op jit(solution)/shard_map/while/body/dot_general | solution.py:73
  49.0 5.8 %convolution_add_fusion.4 = f32[512,512]{1,0:T(8,128)} fusion(f32[512,512]{1,0:T(8,128)S(1)} %fusion.156, bf16[512,512]{1,0:T(8,128)(2,1)S(1)} %convolution_convert_fusion.9), kind=kOutput, calls=%fused_computation.7.clone.1 | convolution fusion | flops 272891904 | bytes 2621440 | tf_op jit(solution)/shard_map/while/body/dot_general | solution.py:77
  54.7 5.0 %fusion.154 = f32[512,512]{1,0:T(8,128)S(1)} fusion(bf16[512,512]{1,0:T(8,128)(2,1)S(1)} %convolution_convert_fusion.8), kind=kOutput, calls=%fused_computation.28.clone.1 | convolution fusion | flops 272629760 | bytes 1572864 | tf_op jit(solution)/shard_map/while/body/dot_general | solution.py:74
  59.7 5.8 %convolution_subtract_fusion.6 = f32[512,512]{1,0:T(8,128)} fusion(f32[512,512]{1,0:T(8,128)S(1)} %fusion.154, bf16[512,512]{1,0:T(8,128)(2,1)S(1)} %convolution_convert_fusion.9), kind=kOutput, calls=%fused_computation.9.clone.1 | convolution fusion | flops 273154048 | bytes 2621440 | tf_op jit(solution)/shard_map/while/body/dot_general | solution.py:74
  65.6 0.1 reshape.158
  65.6 1.1 convolution_convert_fusion.10
  66.7 1.4 fusion.155
  68.2 1.1 convolution_convert_fusion.11
  69.3 1.5 convolution_subtract_fusion.7
  70.8 0.0 copy-start.3
  70.8 1.5 fusion.157
  72.3 0.6 dynamic_slice.63
  72.9 0.7 dynamic_slice.64
  73.5 0.0 copy-done.3
  73.5 3.4 %multiply_add_fusion.4 = (f32[512,512]{1,0:T(8,128)S(1)}, f32[512,512]{1,0:T(8,128)S(1)}, f32[512,512]{1,0:T(8,128)S(1)}) fusion(f32[512,512]{1,0:T(8,128)S(1)} %get-tuple-element.349, f32[512,512]{1,0:T(8,128)S(1)} %copy-done.4, f32[512,512]{1,0:T(8,128)S(1)} %convolution_subtract_fusion.7, f32[512,512]{1,0:T(8,128)S(1)} %copy-done.3, ...), kind=kOutput, calls=%fused_computation.23.clone.1 | convolution fusion | flops 21217280 | bytes 10518664 | tf_op jit(solution)/shard_map/while/body/dot_general | solution.py:89
  86.2 1.0 copy-done
  87.1 0.3 copy-done.1
  87.5 0.4 copy-done.2
  87.9 0.0 all-reduce.3.cloned.1.call-update
  87.9 3.9 %sine_multiply_fusion = f32[512,512]{1,0:T(8,128)S(1)} fusion(), kind=kLoop, calls=%fused_computation.112 | loop fusion | flops 3932160 | bytes 1048576 | tf_op jit(solution)/shard_map/mul | solution.py:33
  91.7 3.8 %cosine_multiply_fusion = f32[512,512]{1,0:T(8,128)S(1)} fusion(), kind=kLoop, calls=%fused_computation.113 | loop fusion | flops 3932160 | bytes 1048576 | tf_op jit(solution)/shard_map/mul | solution.py:32
  95.6 161.6 %all-reduce.3.cloned.1.call-done = (f32[512,512]{1,0:T(8,128)}, f32[512,512]{1,0:T(8,128)}, f32[512,512]{1,0:T(8,128)}) async-done(((f32[512,512]{1,0:T(8,128)}, f32[512,512]{1,0:T(8,128)}, f32[512,512]{1,0:T(8,128)}), (f32[512,512]{1,0:T(8,128)}, f32[512,512]{1,0:T(8,128)}, f32[512,512]{1,0:T(8,128)})) %all-reduce.3.cloned.1.call-update) | async-done | bytes 3145744 | tf_op jit(solution)/shard_map/psum | solution.py:139
  257.2 4.1 %fusion.91 = f32[512,384]{1,0:T(8,128)S(1)} fusion(f32[512,512]{1,0:T(8,128)S(1)} %sine_multiply_fusion, f32[512,512]{1,0:T(8,128)} %get-tuple-element.245, f32[512,512]{1,0:T(8,128)} %get-tuple-element.246), kind=kOutput, calls=%fused_computation.119 | convolution fusion | flops 1208483840 | bytes 3670016 | tf_op jit(solution)/shard_map/dot_general | solution.py:144
  261.3 2.6 fusion.95
  264.0 2.4 convolution_add_fusion.2
  266.4 2.4 convolution_subtract_fusion.2
  268.8 0.5 fusion.98
  269.3 1.1 fusion.82
  (22 shorter events, 0.1 us)
Async XLA Ops:
  6.5 250.7 %all-reduce.3.cloned.1.call-start = ((), (), s32[]{:S(2)}) async-start(), calls=%async_computation | async-start | bytes 6291456 | tf_op jit(solution)/shard_map/psum | solution.py:139
  7.6 6.9 %copy-start.9 = (f32[2]{0:T(128)S(1)}, f32[2]{0:T(128)}, u32[]{:S(2)}) copy-start(f32[2]{0:T(128)} %param.17) | copy-start | bytes 28
  7.6 6.9 %copy-start.10 = (f32[2]{0:T(128)S(1)}, f32[2]{0:T(128)}, u32[]{:S(2)}) copy-start(f32[2]{0:T(128)} %param.16) | copy-start | bytes 28
  7.6 6.9 %copy-start.7 = (s32[2,2]{1,0:T(2,128)S(1)}, s32[2,2]{1,0:T(2,128)}, u32[]{:S(2)}) copy-start(s32[2,2]{1,0:T(2,128)} %param.12) | copy-start | bytes 52
  7.6 7.1 %copy-start.8 = (s32[2,10,2]{1,2,0:T(2,128)S(1)}, s32[2,10,2]{1,2,0:T(2,128)}, u32[]{:S(2)}) copy-start(s32[2,10,2]{1,2,0:T(2,128)} %param.14) | copy-start | bytes 484
  7.6 7.1 %copy-start.11 = (s32[2]{0:T(128)S(1)}, s32[2]{0:T(128)}, u32[]{:S(2)}) copy-start(s32[2]{0:T(128)} %param.13) | copy-start | bytes 28
  8.9 6.6 %collective-permute-start = (bf16[2,64,384]{2,1,0:T(8,128)(2,1)S(1)}, bf16[2,64,384]{2,1,0:T(8,128)(2,1)S(1)}, u32[]{:S(2)}, u32[]{:S(2)}) collective-permute-start(bf16[2,64,384]{2,1,0:T(8,128)(2,1)S(1)} %get-tuple-element.253), channel_id=1, source_target_pairs={{0,4},{4,8},{8,12},{1,5},{5,9},{9,13},{2,6},{6,10},{10,14},{3,7},{... | collective-permute-start | bytes 294920 | tf_op jit(solution)/shard_map/ppermute | solution.py:19
  12.9 5.4 %collective-permute-start.1 = (bf16[2,64,384]{2,1,0:T(8,128)(2,1)S(1)}, bf16[2,64,384]{2,1,0:T(8,128)(2,1)S(1)}, u32[]{:S(2)}, u32[]{:S(2)}) collective-permute-start(bf16[2,64,384]{2,1,0:T(8,128)(2,1)S(1)} %get-tuple-element.254), channel_id=1, source_target_pairs={{4,0},{8,4},{12,8},{5,1},{9,5},{13,9},{6,2},{10,6},{14,10},{7,3},{... | collective-permute-start | bytes 294920 | tf_op jit(solution)/shard_map/ppermute | solution.py:22
  14.3 9.4 %copy-start.6 = (f32[2,10,1024]{2,0,1:T(2,128)S(1)}, f32[2,10,1024]{2,0,1:T(2,128)}, u32[]{:S(2)}) copy-start(f32[2,10,1024]{2,0,1:T(2,128)} %param.15) | copy-start | bytes 245764
  18.4 6.4 %collective-permute-start.2 = (bf16[2,512,64]{2,1,0:T(8,128)(2,1)S(1)}, bf16[2,512,64]{2,1,0:T(8,128)(2,1)S(1)}, u32[]{:S(2)}, u32[]{:S(2)}) collective-permute-start(bf16[2,512,64]{2,1,0:T(8,128)(2,1)S(1)} %get-tuple-element.251), channel_id=1, source_target_pairs={{0,1},{1,2},{2,3},{4,5},{5,6},{6,7},{8,9},{9,10},{10,11},{12,13},{... | collective-permute-start | bytes 393224 | tf_op jit(solution)/shard_map/ppermute | solution.py:19
  21.5 7.1 %collective-permute-start.3 = (bf16[2,512,64]{2,1,0:T(8,128)(2,1)S(1)}, bf16[2,512,64]{2,1,0:T(8,128)(2,1)S(1)}, u32[]{:S(2)}, u32[]{:S(2)}) collective-permute-start(bf16[2,512,64]{2,1,0:T(8,128)(2,1)S(1)} %get-tuple-element.252), channel_id=1, source_target_pairs={{1,0},{2,1},{3,2},{5,4},{6,5},{7,6},{9,8},{10,9},{11,10},{13,12},{... | collective-permute-start | bytes 393224 | tf_op jit(solution)/shard_map/ppermute | solution.py:22
  39.5 5.0 %copy-start.5 = (bf16[2,512,512]{2,1,0:T(8,128)(2,1)S(1)}, bf16[2,512,512]{2,1,0:T(8,128)(2,1)}, u32[]{:S(2)}) copy-start(bf16[2,512,512]{2,1,0:T(8,128)(2,1)} %get-tuple-element.369) | copy-start | bytes 3145732 | tf_op jit(solution)/shard_map/while
  69.3 4.2 %copy-start.4 = (f32[512,512]{1,0:T(8,128)S(1)}, f32[512,512]{1,0:T(8,128)}, u32[]{:S(2)}) copy-start(f32[512,512]{1,0:T(8,128)} %convolution_subtract_fusion.6) | copy-start | bytes 3145732 | tf_op jit(solution)/shard_map/while
  70.8 2.7 copy-start.3
  86.2 1.0 copy-start
  86.2 1.3 copy-start.1
  86.2 1.7 copy-start.2
  257.2 4.1 %copy-start.12 = (f32[512,512]{1,0:T(8,128)S(1)}, f32[512,512]{1,0:T(8,128)}, u32[]{:S(2)}) copy-start(f32[512,512]{1,0:T(8,128)} %get-tuple-element.246) | copy-start | bytes 3145732
  257.2 4.1 %copy-start.14 = (f32[512,512]{1,0:T(8,128)S(1)}, f32[512,512]{1,0:T(8,128)}, u32[]{:S(2)}) copy-start(f32[512,512]{1,0:T(8,128)} %get-tuple-element.245) | copy-start | bytes 3145732
  261.3 2.6 copy-start.13
Sparse Core Ops, SparseCore 0:
  88.0 169.1 all-reduce.2
where the time goes:
time: 278 us
  waiting for transfers between devices  169 us (61%)
  matrix products  54.6 us (20%)
  between operations  14 us (5%)
  other arithmetic  13.6 us (5%)
  loops' own time  11.9 us (4%)
  starting transfers between devices  9.75 us (4%)
  local copies, waits for them, and re-layouts  4.25 us (2%)
    psum x1, waiting for transfers between devices, body(): sum_re, sum_im, sum_den = lax.psum((num_re, num_im, den), 'exp')  162 us
    another operation x1, loops' own time, body(): lax.fori_loop(0, count, own_step, (zero_plane, zero_plane, zero_plane))  11.9 us
    ppermute x2, starting transfers between devices, padded(): lax.ppermute(lax.slice_in_dim(block, block.shape[dim] - width, None, axis...  7.17 us
    ppermute x2, waiting for transfers between devices, padded(): lax.ppermute(lax.slice_in_dim(block, 0, width, axis=dim), axis, backward)  6.66 us
    dot_general x1, matrix products, image_spectrum(): jnp.dot(half_im, fwd_im.T, preferred_element_type=jnp.float32)  5.79 us
    dot_general x1, matrix products, image_spectrum(): jnp.dot(half_im, fwd_re.T, preferred_element_type=jnp.float32)  5.79 us
  transfers between devices with their start and end apart: 5, of which 4 were waited for; matrix products, arithmetic and copies ran while one was open for 3% of the time, Pallas kernels for 0%

commit v1 on v0

v1 whole, which is shorter than its diff:
```python
import functools
import math

import jax
import jax.numpy as jnp
import ml_dtypes
import numpy as np
from jax import lax
from jax.experimental import pallas as pl
from jax.experimental.pallas import tpu as pltpu
from jax.sharding import PartitionSpec as P

TILE = 512
HALO = 64
PS = 32
NBASIS = 10
CORE = 384
CHIPS = 8
BLK = 16
HALF = CHIPS * BLK
ROWS = HALF + BLK
OUT = CORE // (2 * CHIPS)
PACK = 80
MESH = pl.DeviceIdType.MESH
F32 = jnp.float32
BF16 = jnp.bfloat16


def angles(a, b):
    return (a[:, None] * b[None, :] % TILE) * (2.0 * math.pi / TILE)


@functools.cache
def tables():
    freq = np.arange(TILE)
    pixel = (freq + HALO) % TILE
    offset = np.arange(PS) - PS // 2
    scale = 1.0 / math.sqrt(TILE)

    def bf(x):
        return np.asarray(x, np.float32).astype(ml_dtypes.bfloat16)

    rows = [np.arange(HALF * q, HALF * q + ROWS) for q in range(2)]
    live = [(u <= TILE // 2)[:, None] for u in rows]
    ftab = np.stack(
        [
            np.concatenate([np.cos(angles(u, pixel)) * k, -np.sin(angles(u, pixel)) * k]) * scale
            for u, k in zip(rows, live)
        ]
    )
    wtab = np.concatenate([np.cos(angles(pixel, freq)), -np.sin(angles(pixel, freq))], 1) * scale
    pgt = np.stack(
        [np.concatenate([np.cos(angles(u, offset)) * k, -np.sin(angles(u, offset)) * k]) for u, k in zip(rows, live)]
    )
    cos, sin = np.cos(angles(offset, freq)), np.sin(angles(offset, freq))
    cos, sin = np.tile(cos, (4, 1)), np.tile(sin, (4, 1))
    pgw = np.block([[cos, -sin], [sin, cos]])
    core = np.arange(CORE) + HALO
    cos, sin = np.cos(angles(freq, core)) * scale, np.sin(angles(freq, core)) * scale
    ytab = np.block([[cos, sin], [-sin, cos]])
    xtab = np.zeros((2 * CHIPS, 2, CHIPS * OUT, 4 * BLK))
    for z in range(CHIPS):
        for p in range(2):
            x = np.concatenate([OUT * (2 * t + p) + np.arange(OUT) for t in range(CHIPS)]) + HALO
            for side in range(2):
                q = p ^ side
                u = np.concatenate([q * HALF + BLK * z + np.arange(BLK), TILE // 2 + np.arange(BLK)])
                count = np.where((u == 0) | (u == TILE // 2), 1.0, 2.0)
                count[BLK:] = 0.0
                if z == CHIPS - 1 and q == 1:
                    count[BLK] = 1.0
                xtab[2 * z + p, side, :, : 2 * BLK] = np.cos(angles(x, u)) * scale * count
                xtab[2 * z + p, side, :, 2 * BLK :] = -np.sin(angles(x, u)) * scale * count
    edge = np.arange(HALO)
    dist = np.concatenate([HALO - 1 - edge, edge])
    line = np.sin(0.5 * math.pi * (dist + 0.5) / HALO) ** 2
    taper = np.stack([np.tile(line[:, None], (1, 128)), np.tile(line[None, :], (128, 1))]).astype(np.float32)
    return bf(ftab), bf(wtab), bf(pgt), bf(pgw), bf(ytab), bf(xtab), taper


def monomial(value, power):
    return jnp.where(
        power == 0,
        1.0,
        jnp.where(power == 1, value, jnp.where(power == 2, value * value, value * value * value)),
    )


def dot(a, b):
    return jnp.dot(a, b, preferred_element_type=F32)


def kernel(
    foot, anchor, degree, powers, flux, variance, basis, pgt, taper, stamps, ftab_h, wtab_h, pgw_h, ytab_h, xtab_h,
    out,
    core, rowh, first, last, right, left, ap, ftab, wtab, pgw, ytab, xtab,
    psf_own, psf_sib, psf_all, num_sib_out, num_sib_in, num_own, num_out, num_in, ex_in, ex_sum,
    t_own, t_sib, part_out, part_in,
    load_sem, halo_send, halo_recv, sib_send, sib_recv, psf_send, psf_recv, num_send, num_recv,
    ex_send, ex_recv, part_send, part_recv,
):
    group = lax.axis_index("exp")
    r = lax.axis_index("trow")
    c = lax.axis_index("tcol")
    z = group // 2
    p = group % 2
    sib = {"exp": group + 1 - 2 * p}

    def along(k):
        return 2 * ((z + k) % CHIPS) + p

    def near(dr, dc):
        return {"trow": (r + dr + 4) % 4, "tcol": (c + dc + 4) % 4}

    around = [(-1, 0), (1, 0), (0, -1), (0, 1), (-1, -1), (-1, 1), (1, -1), (1, 1)]
    loads = []
    for i, (src, dst) in enumerate(
        [(stamps, core), (ftab_h, ftab), (wtab_h, wtab), (pgw_h, pgw), (ytab_h, ytab), (xtab_h.at[group], xtab)]
    ):
        load = pltpu.make_async_copy(src, dst, load_sem.at[i])
        load.start()
        loads.append(load)
    barrier = pltpu.get_barrier_semaphore()
    for dr, dc in around:
        pl.semaphore_signal(barrier, inc=1, device_id=near(dr, dc), device_id_type=MESH)
    pl.semaphore_signal(barrier, inc=1, device_id=sib, device_id_type=MESH)
    for k in range(1, CHIPS):
        pl.semaphore_signal(barrier, inc=1, device_id={"exp": along(k)}, device_id_type=MESH)

    def remote(src, dst, send, recv, where):
        copy = pltpu.make_async_remote_copy(
            src_ref=src, dst_ref=dst, send_sem=send, recv_sem=recv, device_id=where, device_id_type=MESH
        )
        copy.start()
        return copy

    loads[0].wait()
    lane = lax.broadcasted_iota(jnp.int32, (CORE, 128), 1)
    low = lane < HALO
    first[...] = jnp.where(
        low, core[0, :, 0:128].astype(F32), pltpu.roll(core[1, :, 0:128].astype(F32), HALO, 1)
    ).astype(BF16)
    last[...] = jnp.where(
        low, pltpu.roll(core[0, :, 256:384].astype(F32), HALO, 1), core[1, :, 256:384].astype(F32)
    ).astype(BF16)
    pl.semaphore_wait(barrier, len(around) + CHIPS)
    top, low_rows = pl.ds(0, HALO), pl.ds(CORE - HALO, HALO)
    at_next, at_prev = pl.ds(CORE, HALO), pl.ds(CORE + HALO, HALO)
    pieces = [
        (core.at[:, top, :], rowh.at[:, pl.ds(0, HALO), :]),
        (core.at[:, low_rows, :], rowh.at[:, pl.ds(HALO, HALO), :]),
        (first, right.at[pl.ds(0, CORE), :]),
        (last, left.at[pl.ds(0, CORE), :]),
        (first.at[top, :], right.at[at_next, :]),
        (last.at[top, :], left.at[at_next, :]),
        (first.at[low_rows, :], right.at[at_prev, :]),
        (last.at[low_rows, :], left.at[at_prev, :]),
    ]
    halos = [
        remote(src, dst, halo_send.at[i], halo_recv.at[i], near(*around[i])) for i, (src, dst) in enumerate(pieces)
    ]

    lane32 = lax.broadcasted_iota(jnp.int32, (PS, 128), 1)
    row32 = lax.broadcasted_iota(jnp.int32, (PS, 128), 0)
    slot32 = lane32 // PS
    fold = jnp.where(
        lax.broadcasted_iota(jnp.int32, (128, 128), 0) % PS == lax.broadcasted_iota(jnp.int32, (128, 128), 1) % PS,
        1.0,
        0.0,
    ).astype(BF16)
    lane16 = lax.broadcasted_iota(jnp.int32, (BLK, 128), 1) // PS
    row16 = lax.broadcasted_iota(jnp.int32, (BLK, 128), 0)
    psf = jnp.zeros((PS, 128), F32)
    wrow = jnp.zeros((BLK, 128), F32)
    wnum = []
    for e in range(2):
        ux = (c * CORE + CORE // 2 - anchor[e, 1]).astype(F32) / (2.0 * CORE)
        uy = (r * CORE + CORE // 2 - anchor[e, 0]).astype(F32) / (2.0 * CORE)
        flat = jnp.zeros((1, PS * PS), F32)
        for k in range(NBASIS):
            px, qy = powers[e, k, 0], powers[e, k, 1]
            term = jnp.where(px + qy <= degree[e], monomial(ux, px) * monomial(uy, qy), 0.0)
            flat = flat + term * basis[e, k : k + 1, :]
        spread = jnp.zeros((PS, 128), F32)
        for t in range(PS * PS // 128):
            spread = jnp.where(
                (row32 // 4 == t) & (slot32 == row32 % 4),
                jnp.broadcast_to(flat[:, 128 * t : 128 * t + 128], (PS, 128)),
                spread,
            )
        mine = 2 * p + e
        psf = jnp.where(slot32 == mine, dot(spread.astype(BF16), fold), psf)
        active = (foot[e, 0] <= r) & (r < foot[e, 1]) & (foot[e, 2] <= c) & (c < foot[e, 3])
        gain = jnp.where(active, flux[e], 0.0)
        wnum.append(jnp.full((8, 128), gain, F32) / jnp.full((8, 128), variance[e], F32))
        wden = jnp.full((BLK, 128), gain * flux[e], F32) / jnp.full((BLK, 128), variance[e], F32)
        wrow = jnp.where(lane16 == mine, wden, wrow)
    high = wrow.astype(BF16).astype(F32)
    rest = wrow - high
    mid = rest.astype(BF16).astype(F32)
    wrow = jnp.where(row16 == 0, high, jnp.where(row16 == 1, mid, jnp.where(row16 == 2, rest - mid, 0.0)))
    psf_own[0:PS, :] = psf.astype(BF16)
    psf_own[PS : PS + BLK, :] = wrow.astype(BF16)
    psf_pair = remote(psf_own, psf_sib, sib_send.at[0], sib_recv.at[0], sib)

    for load in loads[1:4]:
        load.wait()
    psf_pair.wait()
    psf_all[0] = (psf_own[...].astype(F32) + psf_sib[...].astype(F32)).astype(BF16)
    psf_copies = [
        remote(psf_all.at[0], psf_all.at[k], psf_send.at[k], psf_recv.at[k], {"exp": along(k)})
        for k in range(1, CHIPS)
    ]

    for copy in halos:
        copy.wait()
    cover = []
    for e in range(2):
        cover.append(
            [
                jnp.where((foot[e, lo] <= at) & (at < foot[e, lo + 1]), 1.0, 0.0)
                for lo, at in ((0, r + 1), (0, r - 1), (2, c + 1), (2, c - 1))
            ]
        )
    lane_s = lax.broadcasted_iota(jnp.int32, (TILE, 128), 1) < HALO
    line_r = taper[0]
    line_c = taper[1]
    right_v, left_v = right[...].astype(F32), left[...].astype(F32)
    right_t, left_t = pltpu.roll(right_v, HALO, 1), pltpu.roll(left_v, HALO, 1)
    for e in range(2):
        ap[e, 0:CORE, 0:CORE] = core[e]
        up, down, after, before = cover[e]
        wide = jnp.concatenate([line_r] * 3, axis=1)
        ap[e, CORE : CORE + HALO, 0:CORE] = (rowh[e, 0:HALO, :].astype(F32) * (wide[0:HALO] * up)).astype(BF16)
        ap[e, CORE + HALO : TILE, 0:CORE] = (rowh[e, HALO:, :].astype(F32) * (wide[HALO:] * down)).astype(BF16)
        side = jnp.where(lane_s, right_v, left_t) if e == 0 else jnp.where(lane_s, right_t, left_v)
        keep = jnp.where(lane_s[0:128], after, before) * line_c
        for t in range(3):
            ap[e, 128 * t : 128 * t + 128, CORE:TILE] = (side[128 * t : 128 * t + 128] * keep).astype(BF16)
        corner = side[CORE:TILE]
        taper2 = line_r * line_c * jnp.where(lane_s[0:128], after, before)
        ap[e, CORE : CORE + HALO, CORE:TILE] = (corner[0:HALO] * (taper2[0:HALO] * up)).astype(BF16)
        ap[e, CORE + HALO : TILE, CORE:TILE] = (corner[HALO:] * (taper2[HALO:] * down)).astype(BF16)

    lane_r = lax.broadcasted_iota(jnp.int32, (2 * ROWS, 128), 1) // PS
    stamp = psf_own[0:PS, :]

    def numerator(q):
        f = ftab[q]
        lift = dot(pgt[q], stamp)
        total_re = total_im = None
        for e in range(2):
            half = dot(f, ap[e]).astype(BF16)
            prod = dot(half, wtab[...])
            spec_re = prod[:ROWS, :TILE] - prod[ROWS:, TILE:]
            spec_im = prod[:ROWS, TILE:] + prod[ROWS:, :TILE]
            one = jnp.where(lane_r == 2 * p + e, lift, 0.0).astype(BF16)
            otf = dot(jnp.concatenate([one[:ROWS], one[ROWS:]], axis=1), pgw[...])
            otf_re, otf_im = otf[:, :TILE], otf[:, TILE:]
            w = wnum[e][0:1, 0:1]
            part_re = w * (otf_re * spec_re + otf_im * spec_im)
            part_im = w * (otf_re * spec_im - otf_im * spec_re)
            total_re = part_re if e == 0 else total_re + part_re
            total_im = part_im if e == 0 else total_im + part_im
        return total_re, total_im

    num_re, num_im = numerator(1 - p)
    num_sib_out[0] = num_re.astype(BF16)
    num_sib_out[1] = num_im.astype(BF16)
    num_pair = remote(num_sib_out, num_sib_in, sib_send.at[1], sib_recv.at[1], sib)
    num_re, num_im = numerator(p)
    num_pair.wait()
    num_re = num_re + num_sib_in[0].astype(F32)
    num_im = num_im + num_sib_in[1].astype(F32)
    num_own[0] = num_re
    num_own[1] = num_im
    num_out[0] = num_re.astype(BF16)
    num_out[1] = num_im.astype(BF16)
    num_copies = [
        remote(
            num_out.at[:, pl.ds(pl.multiple_of(BLK * ((z + k) % CHIPS), BLK), BLK), :],
            num_in.at[k],
            num_send.at[k],
            num_recv.at[k],
            {"exp": along(k)},
        )
        for k in range(1, CHIPS)
    ]

    def extra(at):
        return pltpu.make_async_remote_copy(
            src_ref=num_out.at[:, pl.ds(HALF, BLK), :],
            dst_ref=ex_in.at[at],
            send_sem=ex_send,
            recv_sem=ex_recv.at[at],
            device_id={"exp": 2 * CHIPS - 1},
            device_id_type=MESH,
        )

    @pl.when((p == 1) & (z < CHIPS - 1))
    def _():
        extra(z).start()

    for copy in psf_copies:
        copy.wait()
    start = pl.multiple_of(BLK * z, BLK)
    pgz = jnp.concatenate(
        [
            pgt[p, pl.ds(start, BLK), :],
            pgt[p, HALF:ROWS, :],
            pgt[p, pl.ds(pl.multiple_of(start + ROWS, BLK), BLK), :],
            pgt[p, ROWS + HALF :, :],
        ],
        axis=0,
    )
    lane_d = lax.broadcasted_iota(jnp.int32, (4 * BLK, 128), 1) // PS

    def add_den(g, den):
        lift = dot(pgz, psf_all[g, 0:PS, :])
        weights = jnp.sum(psf_all[g, PS : PS + BLK, :].astype(F32), axis=0, keepdims=True)
        ones = [jnp.where(lane_d == t, lift, 0.0).astype(BF16) for t in range(4)]
        lhs = jnp.concatenate(
            [jnp.concatenate([one[: 2 * BLK], one[2 * BLK :]], axis=1) for one in ones], axis=0
        )
        otf = dot(lhs, pgw[...])
        power = otf[:, :TILE] * otf[:, :TILE] + otf[:, TILE:] * otf[:, TILE:]
        for t in range(4):
            den = den + weights[:, PS * t : PS * t + 1] * power[2 * BLK * t : 2 * BLK * (t + 1)]
        return den

    den = lax.fori_loop(0, CHIPS, add_den, jnp.zeros((2 * BLK, TILE), F32))

    ex_sum[...] = jnp.zeros_like(ex_sum)

    @pl.when(group == 2 * CHIPS - 1)
    def _():
        for t in range(CHIPS - 1):
            extra(t).wait_recv()
        total = num_own[:, HALF:ROWS, :]
        for t in range(CHIPS - 1):
            total = total + ex_in[t].astype(F32)
        ex_sum[...] = total

    sums = num_own[:, pl.ds(start, BLK), :]
    for k in range(1, CHIPS):
        num_copies[k - 1].wait_recv()
        sums = sums + num_in[k].astype(F32)
    norm = lax.rsqrt(den + 1.0)
    s_re = jnp.concatenate([sums[0], ex_sum[0]], axis=0) * norm
    s_im = jnp.concatenate([sums[1], ex_sum[1]], axis=0) * norm
    loads[4].wait()
    loads[5].wait()
    t_all = dot(jnp.concatenate([s_re, s_im], axis=1).astype(BF16), ytab[...])
    t_own[0 : 2 * BLK, :] = t_all[:, :CORE].astype(BF16)
    t_own[2 * BLK :, :] = t_all[:, CORE:].astype(BF16)
    t_pair = remote(t_own, t_sib, sib_send.at[2], sib_recv.at[2], sib)
    image = dot(xtab[0], t_own[...])
    t_pair.wait()
    image = image + dot(xtab[1], t_sib[...])
    for t in range(CHIPS):
        block = image[OUT * t : OUT * (t + 1)]
        part_out[t] = jnp.concatenate(
            [block[:, 128 * i : 128 * i + 128] for i in range(3)] + [jnp.zeros((PACK - 3 * OUT, 128), F32)], axis=0
        ).astype(BF16)
    parts = [
        remote(
            part_out.at[(z + k) % CHIPS], part_in.at[k], part_send.at[k], part_recv.at[k], {"exp": along(k)}
        )
        for k in range(1, CHIPS)
    ]
    total = part_out[z].astype(F32)
    for k in range(1, CHIPS):
        parts[k - 1].wait_recv()
        total = total + part_in[k].astype(F32)
    for i in range(3):
        out[0, :, 128 * i : 128 * i + 128] = total[OUT * i : OUT * (i + 1)]
    for copy in num_copies + parts:
        copy.wait_send()

    @pl.when((p == 1) & (z < CHIPS - 1))
    def _():
        extra(z).wait_send()


def body(stamps, footprint, psf_anchor, psf_degree, psf_powers, psf_basis, flux, variance):
    ftab, wtab, pgt, pgw, ytab, xtab, taper = (jnp.asarray(t) for t in tables())
    smem = pl.BlockSpec(memory_space=pltpu.SMEM)
    vmem = pl.BlockSpec(memory_space=pltpu.VMEM)
    hbm = pl.BlockSpec(memory_space=pl.ANY)
    dma = pltpu.SemaphoreType.DMA
    return pl.pallas_call(
        kernel,
        out_shape=jax.ShapeDtypeStruct((1, OUT, CORE), F32),
        in_specs=[smem] * 6 + [vmem] * 3 + [hbm] * 6,
        out_specs=vmem,
        scratch_shapes=[
            pltpu.VMEM((2, CORE, CORE), BF16),
            pltpu.VMEM((2, 2 * HALO, CORE), BF16),
            pltpu.VMEM((CORE, 128), BF16),
            pltpu.VMEM((CORE, 128), BF16),
            pltpu.VMEM((TILE, 128), BF16),
            pltpu.VMEM((TILE, 128), BF16),
            pltpu.VMEM((2, TILE, TILE), BF16),
            pltpu.VMEM(ftab.shape, BF16),
            pltpu.VMEM(wtab.shape, BF16),
            pltpu.VMEM(pgw.shape, BF16),
            pltpu.VMEM(ytab.shape, BF16),
            pltpu.VMEM(xtab.shape[1:], BF16),
            pltpu.VMEM((PS + BLK, 128), BF16),
            pltpu.VMEM((PS + BLK, 128), BF16),
            pltpu.VMEM((CHIPS, PS + BLK, 128), BF16),
            pltpu.VMEM((2, ROWS, TILE), BF16),
            pltpu.VMEM((2, ROWS, TILE), BF16),
            pltpu.VMEM((2, ROWS, TILE), F32),
            pltpu.VMEM((2, ROWS, TILE), BF16),
            pltpu.VMEM((CHIPS, 2, BLK, TILE), BF16),
            pltpu.VMEM((CHIPS - 1, 2, BLK, TILE), BF16),
            pltpu.VMEM((2, BLK, TILE), F32),
            pltpu.VMEM((4 * BLK, CORE), BF16),
            pltpu.VMEM((4 * BLK, CORE), BF16),
            pltpu.VMEM((CHIPS, PACK, 128), BF16),
            pltpu.VMEM((CHIPS, PACK, 128), BF16),
            dma((6,)),
            dma((8,)),
            dma((8,)),
            dma((3,)),
            dma((3,)),
            dma((CHIPS,)),
            dma((CHIPS,)),
            dma((CHIPS,)),
            dma((CHIPS,)),
            dma,
            dma((CHIPS - 1,)),
            dma((CHIPS,)),
            dma((CHIPS,)),
        ],
        compiler_params=pltpu.CompilerParams(
            collective_id=0, has_side_effects=True, vmem_limit_bytes=48 * 1024 * 1024
        ),
    )(
        footprint, psf_anchor, psf_degree, psf_powers, flux, variance, psf_basis, pgt, taper,
        stamps, ftab, wtab, pgw, ytab, xtab,
    )


def solution(mesh):
    in_specs = (
        P("exp", "trow", "tcol"),
        P("exp", None),
        P("exp", None),
        P("exp"),
        P("exp", None, None),
        P("exp", None, None),
        P("exp"),
        P("exp"),
    )
    out_specs = P("trow", "exp", "tcol")
    return jax.shard_map(body, mesh=mesh, in_specs=in_specs, out_specs=out_specs, check_vma=False)
```

time: 278 us -> 52.6 us (0.19)
  waiting for transfers between devices: 169 us -> 0 us
  matrix products: 54.6 us -> 0 us
  Pallas kernels: 0 us -> 38.8 us
  between operations: 14 us -> 0.03 us
  other arithmetic: 13.6 us -> 0 us
  loops' own time: 11.9 us -> 0 us
  starting transfers between devices: 9.75 us -> 0 us
  local copies, waits for them, and re-layouts: 4.25 us -> 13.2 us
    psum x1 -> x0, waiting for transfers between devices: 162 us -> none  [body(): sum_re, sum_im, sum_den = lax.psum((num_re, num_im, den), 'exp')]
    dot_general x18 -> x0, matrix products: 54.6 us -> none  [the longest x1 5.79 us: image_spectrum(): jnp.dot(half_im, fwd_im.T, preferred_element_type=jnp.float32)]
    pallas_call x0 -> x1, Pallas kernels: none -> 38.8 us  [body(): pl.pallas_call(kernel, out_shape=jax.ShapeDtypeStruct((1, OUT, CORE), F32...]
    another operation x1 -> x0, loops' own time: 11.9 us -> none  [body(): lax.fori_loop(0, count, own_step, (zero_plane, zero_plane, zero_plane))]
    unnamed x24 -> x27, local copies, waits for them, and re-layouts: 1.72 us -> 13.2 us
    ppermute x4 -> x0, starting transfers between devices: 9.75 us -> none  [the longest x2 7.17 us: padded(): lax.ppermute(lax.slice_in_dim(block, block.shape[dim] - width, None, axis...]
    mul x5 -> x0, other arithmetic: 8.16 us -> none  [the longest x1 3.86 us: spectral_tables(): sine = jnp.sin(angle) * scale]
    ppermute x4 -> x0, waiting for transfers between devices: 7.74 us -> none  [the longest x2 6.66 us: padded(): lax.ppermute(lax.slice_in_dim(block, 0, width, axis=dim), axis, backward)]
  transfers between devices with their start and end apart: 5 -> 0, of which waited for: 4 -> 0; matrix products, arithmetic and copies ran while one was open for 3% -> 0% of each run, Pallas kernels for 0% -> 0%
where the time goes in v1:
time: 52.6 us; the launch traced here: 52.1 us
  Pallas kernels  38.8 us (74%)
  local copies, waits for them, and re-layouts  13.2 us (25%)
    pallas_call x1, Pallas kernels, body(): pl.pallas_call(kernel, out_shape=jax.ShapeDtypeStruct((1, OUT, CORE), F32...  38.8 us
    unnamed x27, local copies, waits for them, and re-layouts  13.2 us

profile of v1, /device:TPU:1, one launch (start us, length us, event | category | flops | bytes accessed | tf_op | source)
XLA Modules:
  0.0 52.1 jit_solution(3866552130032926713)
XLA Ops:
  0.0 0.8 %copy.16.powers = s32[2,10,2]{2,1,0:T(8,128)S(1)} copy(s32[2,10,2]{1,2,0:T(2,128)} %param.19) | data formatting | bytes 320 | tf_op args[4]
  0.8 0.9 %copy.17.basis = f32[2,10,1024]{2,1,0:T(8,128)S(1)} copy(f32[2,10,1024]{2,0,1:T(2,128)} %param.20) | data formatting | bytes 163840 | tf_op args[5]
  1.7 0.0 copy-start
  1.7 1.4 %copy-done = bf16[1024,768]{1,0:T(8,128)(2,1)S(1)} copy-done((bf16[1024,768]{1,0:T(8,128)(2,1)S(1)}, bf16[1024,768]{1,0:T(8,128)(2,1)}, u32[]{:S(2)}) %copy-start) | copy-done | bytes 1572888
  3.1 0.0 copy-start.1
  3.1 1.2 %copy-done.1 = bf16[512,1024]{1,0:T(8,128)(2,1)S(1)} copy-done((bf16[512,1024]{1,0:T(8,128)(2,1)S(1)}, bf16[512,1024]{1,0:T(8,128)(2,1)}, u32[]{:S(2)}) %copy-start.1) | copy-done | bytes 1048600
  4.3 0.0 copy-start.2
  4.3 1.1 %copy-done.2 = bf16[2,384,384]{2,1,0:T(8,128)(2,1)S(1)} copy-done((bf16[2,384,384]{2,1,0:T(8,128)(2,1)S(1)}, bf16[2,384,384]{2,1,0:T(8,128)(2,1)}, u32[]{:S(2)}) %copy-start.2) | copy-done | bytes 589848
  5.4 0.0 copy-start.3
  5.4 1.1 %copy-done.3 = bf16[2,288,512]{2,1,0:T(8,128)(2,1)S(1)} copy-done((bf16[2,288,512]{2,1,0:T(8,128)(2,1)S(1)}, bf16[2,288,512]{2,1,0:T(8,128)(2,1)}, u32[]{:S(2)}) %copy-start.3) | copy-done | bytes 589848
  6.5 0.0 copy-start.4
  6.5 1.0 %copy-done.4 = bf16[256,1024]{1,0:T(8,128)(2,1)S(1)} copy-done((bf16[256,1024]{1,0:T(8,128)(2,1)S(1)}, bf16[256,1024]{1,0:T(8,128)(2,1)}, u32[]{:S(2)}) %copy-start.4) | copy-done | bytes 524312
  7.5 0.0 copy-start.5
  7.5 0.9 %copy-done.5 = bf16[2,288,32]{2,1,0:T(8,128)(2,1)S(1)} copy-done((bf16[2,288,32]{2,1,0:T(8,128)(2,1)S(1)}, bf16[2,288,32]{2,1,0:T(8,128)(2,1)}, u32[]{:S(2)}) %copy-start.5) | copy-done | bytes 36888
  8.4 0.0 copy-start.6
  8.4 0.9 %copy-done.6 = f32[2,128,128]{2,1,0:T(8,128)S(1)} copy-done((f32[2,128,128]{2,1,0:T(8,128)S(1)}, f32[2,128,128]{2,1,0:T(8,128)}, u32[]{:S(2)}) %copy-start.6) | copy-done | bytes 131096
  9.3 0.0 copy-start.7
  9.3 0.7 %copy-done.7 = s32[2,4]{1,0:T(2,128)S(1)} copy-done((s32[2,4]{1,0:T(2,128)S(1)}, s32[2,4]{1,0:T(2,128)}, u32[]{:S(2)}) %copy-start.7) | copy-done | bytes 56
  10.0 0.0 copy-start.8
  10.0 0.7 %copy-done.8 = s32[2,2]{1,0:T(2,128)S(1)} copy-done((s32[2,2]{1,0:T(2,128)S(1)}, s32[2,2]{1,0:T(2,128)}, u32[]{:S(2)}) %copy-start.8) | copy-done | bytes 40
  10.7 0.0 copy-start.9
  10.7 0.7 %copy-done.9 = s32[2]{0:T(128)S(1)} copy-done((s32[2]{0:T(128)S(1)}, s32[2]{0:T(128)}, u32[]{:S(2)}) %copy-start.9) | copy-done | bytes 32
  11.3 0.0 copy-start.10
  11.3 0.7 %copy-done.10 = f32[2]{0:T(128)S(1)} copy-done((f32[2]{0:T(128)S(1)}, f32[2]{0:T(128)}, u32[]{:S(2)}) %copy-start.10) | copy-done | bytes 32
  12.0 0.0 copy-start.11
  12.0 0.7 %copy-done.11 = f32[2]{0:T(128)S(1)} copy-done((f32[2]{0:T(128)S(1)}, f32[2]{0:T(128)}, u32[]{:S(2)}) %copy-start.11) | copy-done | bytes 32
  12.6 38.8 %shard_map.145 = f32[1,24,384]{2,1,0:T(8,128)S(1)} custom-call(s32[2,4]{1,0:T(2,128)S(1)} %copy-done.7, s32[2,2]{1,0:T(2,128)S(1)} %copy-done.8, s32[2]{0:T(128)S(1)} %copy-done.9, s32[2,10,2]{2,1,0:T(8,128)S(1)} %copy.16.powers, f32[2]{0:T(128)S(1)} %copy-done.10, f32[2]{0:T(128)S(1)} %copy-done.11, f32[2,10,1024]{2,1,0:T(8,128)S(1)} %copy.17.basis, ...), custom_call_target="tpu_custom_call" | custom-call | tf_op jit(solution)/shard_map/pallas_call | solution.py:391
  51.5 0.6 %copy.19 = f32[1,24,384]{2,1,0:T(8,128)} copy(f32[1,24,384]{2,1,0:T(8,128)S(1)} %shard_map.145) | data formatting | bytes 73728
Async XLA Ops:
  1.7 1.4 %copy-start = (bf16[1024,768]{1,0:T(8,128)(2,1)S(1)}, bf16[1024,768]{1,0:T(8,128)(2,1)}, u32[]{:S(2)}) copy-start(bf16[1024,768]{1,0:T(8,128)(2,1)} %constant.18.clone.ytab_h) | copy-start | bytes 4718596
  3.1 1.2 %copy-start.1 = (bf16[512,1024]{1,0:T(8,128)(2,1)S(1)}, bf16[512,1024]{1,0:T(8,128)(2,1)}, u32[]{:S(2)}) copy-start(bf16[512,1024]{1,0:T(8,128)(2,1)} %constant.15.clone.wtab_h) | copy-start | bytes 3145732
  4.3 1.1 %copy-start.2 = (bf16[2,384,384]{2,1,0:T(8,128)(2,1)S(1)}, bf16[2,384,384]{2,1,0:T(8,128)(2,1)}, u32[]{:S(2)}) copy-start(bf16[2,384,384]{2,1,0:T(8,128)(2,1)} %stamps.1) | copy-start | bytes 1769476
  5.4 1.1 %copy-start.3 = (bf16[2,288,512]{2,1,0:T(8,128)(2,1)S(1)}, bf16[2,288,512]{2,1,0:T(8,128)(2,1)}, u32[]{:S(2)}) copy-start(bf16[2,288,512]{2,1,0:T(8,128)(2,1)} %constant.14.clone.ftab_h) | copy-start | bytes 1769476
  6.5 1.0 %copy-start.4 = (bf16[256,1024]{1,0:T(8,128)(2,1)S(1)}, bf16[256,1024]{1,0:T(8,128)(2,1)}, u32[]{:S(2)}) copy-start(bf16[256,1024]{1,0:T(8,128)(2,1)} %constant.17.clone.pgw_h) | copy-start | bytes 1572868
  7.5 0.9 %copy-start.5 = (bf16[2,288,32]{2,1,0:T(8,128)(2,1)S(1)}, bf16[2,288,32]{2,1,0:T(8,128)(2,1)}, u32[]{:S(2)}) copy-start(bf16[2,288,32]{2,1,0:T(8,128)(2,1)} %constant.16.clone.pgt) | copy-start | bytes 110596
  8.4 0.9 %copy-start.6 = (f32[2,128,128]{2,1,0:T(8,128)S(1)}, f32[2,128,128]{2,1,0:T(8,128)}, u32[]{:S(2)}) copy-start(f32[2,128,128]{2,1,0:T(8,128)} %constant.20.clone.taper) | copy-start | bytes 393220
  9.3 0.7 %copy-start.7 = (s32[2,4]{1,0:T(2,128)S(1)}, s32[2,4]{1,0:T(2,128)}, u32[]{:S(2)}) copy-start(s32[2,4]{1,0:T(2,128)} %foot.1) | copy-start | bytes 100
  10.0 0.7 %copy-start.8 = (s32[2,2]{1,0:T(2,128)S(1)}, s32[2,2]{1,0:T(2,128)}, u32[]{:S(2)}) copy-start(s32[2,2]{1,0:T(2,128)} %anchor.1) | copy-start | bytes 52
  10.7 0.7 %copy-start.9 = (s32[2]{0:T(128)S(1)}, s32[2]{0:T(128)}, u32[]{:S(2)}) copy-start(s32[2]{0:T(128)} %degree.1) | copy-start | bytes 28
  11.3 0.7 %copy-start.10 = (f32[2]{0:T(128)S(1)}, f32[2]{0:T(128)}, u32[]{:S(2)}) copy-start(f32[2]{0:T(128)} %flux.1) | copy-start | bytes 28
  12.0 0.7 %copy-start.11 = (f32[2]{0:T(128)S(1)}, f32[2]{0:T(128)}, u32[]{:S(2)}) copy-start(f32[2]{0:T(128)} %variance.1) | copy-start | bytes 28

commit v2 on v1

--- a/solution.py
+++ b/solution.py
@@ -16,6 +16,8 @@
 NBASIS = 10
 CORE = 384
 CHIPS = 8
+SIDE = TILE // 2
+FAR = (4, 3, 5, 2, 6, 1, 7)
 BLK = 16
 HALF = CHIPS * BLK
 ROWS = HALF + BLK
@@ -48,16 +50,18 @@
             for u, k in zip(rows, live)
         ]
     )
-    wtab = np.concatenate([np.cos(angles(pixel, freq)), -np.sin(angles(pixel, freq))], 1) * scale
+    wtab = np.concatenate([np.cos(angles(pixel, freq[:SIDE])), -np.sin(angles(pixel, freq[:SIDE]))], 1) * scale
+    wtab[:, SIDE] = np.cos(angles(pixel, freq[SIDE : SIDE + 1]))[:, 0] * scale
     pgt = np.stack(
         [np.concatenate([np.cos(angles(u, offset)) * k, -np.sin(angles(u, offset)) * k]) for u, k in zip(rows, live)]
     )
-    cos, sin = np.cos(angles(offset, freq)), np.sin(angles(offset, freq))
+    order = np.concatenate([freq[:SIDE], freq[SIDE : SIDE + 1], freq[:SIDE:-1]])
+    cos, sin = np.cos(angles(offset, order)), np.sin(angles(offset, order))
     cos, sin = np.tile(cos, (4, 1)), np.tile(sin, (4, 1))
     pgw = np.block([[cos, -sin], [sin, cos]])
     core = np.arange(CORE) + HALO
-    cos, sin = np.cos(angles(freq, core)) * scale, np.sin(angles(freq, core)) * scale
-    ytab = np.block([[cos, sin], [-sin, cos]])
+    ytab = np.concatenate([np.cos(angles(freq[:SIDE], core)), np.sin(angles(freq[:SIDE], core))]) * scale
+    ytab[SIDE] = np.cos(angles(freq[SIDE : SIDE + 1], core))[0] * scale
     xtab = np.zeros((2 * CHIPS, 2, CHIPS * OUT, 4 * BLK))
     for z in range(CHIPS):
         for p in range(2):
@@ -91,9 +95,10 @@
 
 
 def kernel(
-    foot, anchor, degree, powers, flux, variance, basis, pgt, taper, stamps, ftab_h, wtab_h, pgw_h, ytab_h, xtab_h,
+    foot_h, anchor_h, degree_h, powers_h, flux_h, variance_h, basis_h, pgt_h, taper_h, stamps, ftab_h, wtab_h, pgw_h,
+    ytab_h, xtab_h,
     out,
-    core, rowh, first, last, right, left, ap, ftab, wtab, pgw, ytab, xtab,
+    foot, anchor, degree, powers, flux, variance, basis, pgt, taper, strip, otf_all, rowh, first, last, right, left, ap, ftab, wtab, pgw, ytab, xtab,
     psf_own, psf_sib, psf_all, num_sib_out, num_sib_in, num_own, num_out, num_in, ex_in, ex_sum,
     t_own, t_sib, part_out, part_in,
     load_sem, halo_send, halo_recv, sib_send, sib_recv, psf_send, psf_recv, num_send, num_recv,
@@ -112,20 +117,26 @@
     def near(dr, dc):
         return {"trow": (r + dr + 4) % 4, "tcol": (c + dc + 4) % 4}
 
-    around = [(-1, 0), (1, 0), (0, -1), (0, 1), (-1, -1), (-1, 1), (1, -1), (1, 1)]
+    around = [(-1, -1), (-1, 1), (1, -1), (1, 1), (0, -1), (0, 1), (-1, 0), (1, 0)]
+    barrier = pltpu.get_barrier_semaphore()
+    for dr, dc in around:
+        pl.semaphore_signal(barrier, inc=1, device_id=near(dr, dc), device_id_type=MESH)
+    for k in FAR:
+        pl.semaphore_signal(barrier, inc=1, device_id={"exp": along(k)}, device_id_type=MESH)
+    pl.semaphore_signal(barrier, inc=1, device_id=sib, device_id_type=MESH)
     loads = []
     for i, (src, dst) in enumerate(
-        [(stamps, core), (ftab_h, ftab), (wtab_h, wtab), (pgw_h, pgw), (ytab_h, ytab), (xtab_h.at[group], xtab)]
+        [
+            (stamps.at[:, :, pl.ds(0, 128)], strip.at[0]), (stamps.at[:, :, pl.ds(CORE - 128, 128)], strip.at[1]),
+            (foot_h, foot), (anchor_h, anchor), (degree_h, degree), (powers_h, powers),
+            (flux_h, flux), (variance_h, variance), (basis_h, basis), (pgt_h, pgt), (pgw_h, pgw),
+            (stamps, ap.at[:, pl.ds(0, CORE), pl.ds(0, CORE)]), (taper_h, taper), (ftab_h, ftab), (wtab_h, wtab),
+            (ytab_h, ytab), (xtab_h.at[group], xtab),
+        ]
     ):
         load = pltpu.make_async_copy(src, dst, load_sem.at[i])
         load.start()
         loads.append(load)
-    barrier = pltpu.get_barrier_semaphore()
-    for dr, dc in around:
-        pl.semaphore_signal(barrier, inc=1, device_id=near(dr, dc), device_id_type=MESH)
-    pl.semaphore_signal(barrier, inc=1, device_id=sib, device_id_type=MESH)
-    for k in range(1, CHIPS):
-        pl.semaphore_signal(barrier, inc=1, device_id={"exp": along(k)}, device_id_type=MESH)
 
     def remote(src, dst, send, recv, where):
         copy = pltpu.make_async_remote_copy(
@@ -135,30 +146,29 @@
         return copy
 
     loads[0].wait()
-    lane = lax.broadcasted_iota(jnp.int32, (CORE, 128), 1)
-    low = lane < HALO
-    first[...] = jnp.where(
-        low, core[0, :, 0:128].astype(F32), pltpu.roll(core[1, :, 0:128].astype(F32), HALO, 1)
-    ).astype(BF16)
-    last[...] = jnp.where(
-        low, pltpu.roll(core[0, :, 256:384].astype(F32), HALO, 1), core[1, :, 256:384].astype(F32)
-    ).astype(BF16)
+    loads[1].wait()
+    low = lax.broadcasted_iota(jnp.int32, (CORE, 128), 1) < HALO
+    first[...] = jnp.where(low, strip[0, 0].astype(F32), pltpu.roll(strip[0, 1].astype(F32), HALO, 1)).astype(BF16)
+    last[...] = jnp.where(low, pltpu.roll(strip[1, 0].astype(F32), HALO, 1), strip[1, 1].astype(F32)).astype(BF16)
     pl.semaphore_wait(barrier, len(around) + CHIPS)
     top, low_rows = pl.ds(0, HALO), pl.ds(CORE - HALO, HALO)
     at_next, at_prev = pl.ds(CORE, HALO), pl.ds(CORE + HALO, HALO)
     pieces = [
-        (core.at[:, top, :], rowh.at[:, pl.ds(0, HALO), :]),
-        (core.at[:, low_rows, :], rowh.at[:, pl.ds(HALO, HALO), :]),
-        (first, right.at[pl.ds(0, CORE), :]),
-        (last, left.at[pl.ds(0, CORE), :]),
         (first.at[top, :], right.at[at_next, :]),
         (last.at[top, :], left.at[at_next, :]),
         (first.at[low_rows, :], right.at[at_prev, :]),
         (last.at[low_rows, :], left.at[at_prev, :]),
+        (first, right.at[pl.ds(0, CORE), :]),
+        (last, left.at[pl.ds(0, CORE), :]),
+        (stamps.at[:, top, :], rowh.at[:, pl.ds(0, HALO), :]),
+        (stamps.at[:, low_rows, :], rowh.at[:, pl.ds(HALO, HALO), :]),
     ]
     halos = [
         remote(src, dst, halo_send.at[i], halo_recv.at[i], near(*around[i])) for i, (src, dst) in enumerate(pieces)
     ]
+
+    for load in loads[2:9]:
+        load.wait()
 
     lane32 = lax.broadcasted_iota(jnp.int32, (PS, 128), 1)
     row32 = lax.broadcasted_iota(jnp.int32, (PS, 128), 0)
@@ -178,9 +188,9 @@
         uy = (r * CORE + CORE // 2 - anchor[e, 0]).astype(F32) / (2.0 * CORE)
         flat = jnp.zeros((1, PS * PS), F32)
         for k in range(NBASIS):
-            px, qy = powers[e, k, 0], powers[e, k, 1]
+            px, qy = powers[e, 0, k], powers[e, 1, k]
             term = jnp.where(px + qy <= degree[e], monomial(ux, px) * monomial(uy, qy), 0.0)
-            flat = flat + term * basis[e, k : k + 1, :]
+            flat = flat + term * basis[k, e : e + 1, :]
         spread = jnp.zeros((PS, 128), F32)
         for t in range(PS * PS // 128):
             spread = jnp.where(
@@ -203,17 +213,27 @@
     psf_own[PS : PS + BLK, :] = wrow.astype(BF16)
     psf_pair = remote(psf_own, psf_sib, sib_send.at[0], sib_recv.at[0], sib)
 
-    for load in loads[1:4]:
+
+    loads[9].wait()
+    loads[10].wait()
+    stamp = psf_own[0:PS, :]
+    lane_r = lax.broadcasted_iota(jnp.int32, (2 * ROWS, 128), 1) // PS
+    for side in range(2):
+        lift = dot(pgt[1 - p if side == 0 else p], stamp)
+        for e in range(2):
+            one = jnp.where(lane_r == 2 * p + e, lift, 0.0).astype(BF16)
+            otf_all[side, e] = dot(jnp.concatenate([one[:ROWS], one[ROWS:]], axis=1), pgw[...])
+        if side == 0:
+            psf_pair.wait_recv()
+            psf_all[0] = (psf_own[...].astype(F32) + psf_sib[...].astype(F32)).astype(BF16)
+            psf_copies = [
+                remote(psf_all.at[0], psf_all.at[k], psf_send.at[k], psf_recv.at[k], {"exp": along(k)}) for k in FAR
+            ]
+
+    for load in loads[11:15]:
         load.wait()
-    psf_pair.wait()
-    psf_all[0] = (psf_own[...].astype(F32) + psf_sib[...].astype(F32)).astype(BF16)
-    psf_copies = [
-        remote(psf_all.at[0], psf_all.at[k], psf_send.at[k], psf_recv.at[k], {"exp": along(k)})
-        for k in range(1, CHIPS)
-    ]
-
     for copy in halos:
-        copy.wait()
+        copy.wait_recv()
     cover = []
     for e in range(2):
         cover.append(
@@ -228,7 +248,6 @@
     right_v, left_v = right[...].astype(F32), left[...].astype(F32)
     right_t, left_t = pltpu.roll(right_v, HALO, 1), pltpu.roll(left_v, HALO, 1)
     for e in range(2):
-        ap[e, 0:CORE, 0:CORE] = core[e]
         up, down, after, before = cover[e]
         wide = jnp.concatenate([line_r] * 3, axis=1)
         ap[e, CORE : CORE + HALO, 0:CORE] = (rowh[e, 0:HALO, :].astype(F32) * (wide[0:HALO] * up)).astype(BF16)
@@ -242,21 +261,22 @@
         ap[e, CORE : CORE + HALO, CORE:TILE] = (corner[0:HALO] * (taper2[0:HALO] * up)).astype(BF16)
         ap[e, CORE + HALO : TILE, CORE:TILE] = (corner[HALO:] * (taper2[HALO:] * down)).astype(BF16)
 
-    lane_r = lax.broadcasted_iota(jnp.int32, (2 * ROWS, 128), 1) // PS
-    stamp = psf_own[0:PS, :]
-
-    def numerator(q):
-        f = ftab[q]
-        lift = dot(pgt[q], stamp)
+    lane0 = lax.broadcasted_iota(jnp.int32, (ROWS, SIDE), 1) == 0
+
+    def numerator(q, side):
         total_re = total_im = None
         for e in range(2):
-            half = dot(f, ap[e]).astype(BF16)
+            half = dot(ftab[q], ap[e]).astype(BF16)
             prod = dot(half, wtab[...])
-            spec_re = prod[:ROWS, :TILE] - prod[ROWS:, TILE:]
-            spec_im = prod[:ROWS, TILE:] + prod[ROWS:, :TILE]
-            one = jnp.where(lane_r == 2 * p + e, lift, 0.0).astype(BF16)
-            otf = dot(jnp.concatenate([one[:ROWS], one[ROWS:]], axis=1), pgw[...])
-            otf_re, otf_im = otf[:, :TILE], otf[:, TILE:]
+            re_cos, re_sin = prod[:ROWS, :SIDE], prod[:ROWS, SIDE:]
+            im_cos, im_sin = prod[ROWS:, :SIDE], prod[ROWS:, SIDE:]
+            spec_re = jnp.concatenate(
+                [re_cos - jnp.where(lane0, 0.0, im_sin), jnp.where(lane0, re_sin, re_cos + im_sin)], axis=1
+            )
+            spec_im = jnp.concatenate(
+                [im_cos + jnp.where(lane0, 0.0, re_sin), jnp.where(lane0, im_sin, im_cos - re_sin)], axis=1
+            )
+            otf_re, otf_im = otf_all[side, e, :, :TILE], otf_all[side, e, :, TILE:]
             w = wnum[e][0:1, 0:1]
             part_re = w * (otf_re * spec_re + otf_im * spec_im)
             part_im = w * (otf_re * spec_im - otf_im * spec_re)
@@ -264,12 +284,12 @@
             total_im = part_im if e == 0 else total_im + part_im
         return total_re, total_im
 
-    num_re, num_im = numerator(1 - p)
+    num_re, num_im = numerator(1 - p, 0)
     num_sib_out[0] = num_re.astype(BF16)
     num_sib_out[1] = num_im.astype(BF16)
     num_pair = remote(num_sib_out, num_sib_in, sib_send.at[1], sib_recv.at[1], sib)
-    num_re, num_im = numerator(p)
-    num_pair.wait()
+    num_re, num_im = numerator(p, 1)
+    num_pair.wait_recv()
     num_re = num_re + num_sib_in[0].astype(F32)
     num_im = num_im + num_sib_in[1].astype(F32)
     num_own[0] = num_re
@@ -284,7 +304,7 @@
             num_recv.at[k],
             {"exp": along(k)},
         )
-        for k in range(1, CHIPS)
+        for k in FAR
     ]
 
     def extra(at):
@@ -302,7 +322,7 @@
         extra(z).start()
 
     for copy in psf_copies:
-        copy.wait()
+        copy.wait_recv()
     start = pl.multiple_of(BLK * z, BLK)
     pgz = jnp.concatenate(
         [
@@ -342,20 +362,23 @@
         ex_sum[...] = total
 
     sums = num_own[:, pl.ds(start, BLK), :]
-    for k in range(1, CHIPS):
-        num_copies[k - 1].wait_recv()
+    for k, copy in reversed(list(zip(FAR, num_copies))):
+        copy.wait_recv()
         sums = sums + num_in[k].astype(F32)
     norm = lax.rsqrt(den + 1.0)
     s_re = jnp.concatenate([sums[0], ex_sum[0]], axis=0) * norm
     s_im = jnp.concatenate([sums[1], ex_sum[1]], axis=0) * norm
-    loads[4].wait()
-    loads[5].wait()
-    t_all = dot(jnp.concatenate([s_re, s_im], axis=1).astype(BF16), ytab[...])
-    t_own[0 : 2 * BLK, :] = t_all[:, :CORE].astype(BF16)
-    t_own[2 * BLK :, :] = t_all[:, CORE:].astype(BF16)
+    loads[15].wait()
+    loads[16].wait()
+    lane0 = lax.broadcasted_iota(jnp.int32, (2 * BLK, SIDE), 1) == 0
+    (re_p, re_m), (im_p, im_m) = ((x[:, :SIDE], x[:, SIDE:]) for x in (s_re, s_im))
+    top_rows = [jnp.where(lane0, re_p, re_p + re_m), jnp.where(lane0, re_m, im_m - im_p)]
+    low_rows = [jnp.where(lane0, im_p, im_p + im_m), jnp.where(lane0, im_m, re_p - re_m)]
+    folded = jnp.concatenate([jnp.concatenate(top_rows, axis=1), jnp.concatenate(low_rows, axis=1)], axis=0)
+    t_own[...] = dot(folded.astype(BF16), ytab[...]).astype(BF16)
     t_pair = remote(t_own, t_sib, sib_send.at[2], sib_recv.at[2], sib)
     image = dot(xtab[0], t_own[...])
-    t_pair.wait()
+    t_pair.wait_recv()
     image = image + dot(xtab[1], t_sib[...])
     for t in range(CHIPS):
         block = image[OUT * t : OUT * (t + 1)]
@@ -366,15 +389,15 @@
         remote(
             part_out.at[(z + k) % CHIPS], part_in.at[k], part_send.at[k], part_recv.at[k], {"exp": along(k)}
         )
-        for k in range(1, CHIPS)
+        for k in FAR
     ]
     total = part_out[z].astype(F32)
-    for k in range(1, CHIPS):
-        parts[k - 1].wait_recv()
+    for k, copy in reversed(list(zip(FAR, parts))):
+        copy.wait_recv()
         total = total + part_in[k].astype(F32)
     for i in range(3):
         out[0, :, 128 * i : 128 * i + 128] = total[OUT * i : OUT * (i + 1)]
-    for copy in num_copies + parts:
+    for copy in halos + psf_copies + [psf_pair, num_pair, t_pair] + num_copies + parts:
         copy.wait_send()
 
     @pl.when((p == 1) & (z < CHIPS - 1))
@@ -384,17 +407,26 @@
 
 def body(stamps, footprint, psf_anchor, psf_degree, psf_powers, psf_basis, flux, variance):
     ftab, wtab, pgt, pgw, ytab, xtab, taper = (jnp.asarray(t) for t in tables())
-    smem = pl.BlockSpec(memory_space=pltpu.SMEM)
     vmem = pl.BlockSpec(memory_space=pltpu.VMEM)
     hbm = pl.BlockSpec(memory_space=pl.ANY)
     dma = pltpu.SemaphoreType.DMA
     return pl.pallas_call(
         kernel,
         out_shape=jax.ShapeDtypeStruct((1, OUT, CORE), F32),
-        in_specs=[smem] * 6 + [vmem] * 3 + [hbm] * 6,
+        in_specs=[hbm] * 15,
         out_specs=vmem,
         scratch_shapes=[
-            pltpu.VMEM((2, CORE, CORE), BF16),
+            pltpu.SMEM((2, 4), jnp.int32),
+            pltpu.SMEM((2, 2), jnp.int32),
+            pltpu.SMEM((2,), jnp.int32),
+            pltpu.SMEM((2, 2, NBASIS), jnp.int32),
+            pltpu.SMEM((2,), F32),
+            pltpu.SMEM((2,), F32),
+            pltpu.VMEM((NBASIS, 2, PS * PS), F32),
+            pltpu.VMEM(pgt.shape, BF16),
+            pltpu.VMEM(taper.shape, F32),
+            pltpu.VMEM((2, 2, CORE, 128), BF16),
+            pltpu.VMEM((2, 2, ROWS, 2 * TILE), F32),
             pltpu.VMEM((2, 2 * HALO, CORE), BF16),
             pltpu.VMEM((CORE, 128), BF16),
             pltpu.VMEM((CORE, 128), BF16),
@@ -420,7 +452,7 @@
             pltpu.VMEM((4 * BLK, CORE), BF16),
             pltpu.VMEM((CHIPS, PACK, 128), BF16),
             pltpu.VMEM((CHIPS, PACK, 128), BF16),
-            dma((6,)),
+            dma((17,)),
             dma((8,)),
             dma((8,)),
             dma((3,)),
@@ -435,10 +467,11 @@
             dma((CHIPS,)),
         ],
         compiler_params=pltpu.CompilerParams(
-            collective_id=0, has_side_effects=True, vmem_limit_bytes=48 * 1024 * 1024
+            collective_id=0, has_side_effects=True, vmem_limit_bytes=64 * 1024 * 1024 - 65536
         ),
     )(
-        footprint, psf_anchor, psf_degree, psf_powers, flux, variance, psf_basis, pgt, taper,
+        footprint, psf_anchor, psf_degree, psf_powers.transpose(0, 2, 1), flux, variance,
+        psf_basis.transpose(1, 0, 2), pgt, taper,
         stamps, ftab, wtab, pgw, ytab, xtab,
     )
 

time: 52.6 us -> 36.4 us (0.69)
  local copies, waits for them, and re-layouts: 13.2 us -> 1.39 us
  Pallas kernels: 38.8 us -> 34.8 us
    unnamed x27 -> x1, local copies, waits for them, and re-layouts: 13.2 us -> 1.39 us
    pallas_call x1, Pallas kernels: 38.8 us -> 34.8 us  [body(): pl.pallas_call(kernel, out_shape=jax.ShapeDtypeStruct((1, OUT, CORE), F32...]
where the time goes in v2:
time: 36.4 us; the launch traced here: 36.2 us
  Pallas kernels  34.8 us (96%)
  local copies, waits for them, and re-layouts  1.39 us (4%)
    pallas_call x1, Pallas kernels, body(): pl.pallas_call(kernel, out_shape=jax.ShapeDtypeStruct((1, OUT, CORE), F32...  34.8 us
    unnamed x1, local copies, waits for them, and re-layouts  1.39 us

profile of v2, /device:TPU:1, one launch (start us, length us, event | category | flops | bytes accessed | tf_op | source)
XLA Modules:
  0.0 36.2 jit_solution(2631168659171478699)
XLA Ops:
  0.0 34.8 %shard_map.145 = f32[1,24,384]{2,1,0:T(8,128)} custom-call(s32[2,4]{1,0:T(2,128)} %foot_h.1, s32[2,2]{1,0:T(2,128)} %anchor_h.1, s32[2]{0:T(128)} %degree_h.1, s32[2,2,10]{2,1,0:T(2,128)} %bitcast.3, f32[2]{0:T(128)} %flux_h.1, f32[2]{0:T(128)} %variance_h.1, f32[10,2,1024]{2,1,0:T(2,128)} %bitcast.2, bf16[2,288,32]{2,1,0:T(8,128)(2,1)} %constant.16.clone.pgt_h, ...), custom_call_target="tpu_custom_call" | custom-call | tf_op jit(solution)/shard_map/pallas_call | solution.py:413
  34.9 1.4 %copy.17 = f32[1,24,384]{2,1,0:T(8,128)} copy(f32[1,24,384]{2,1,0:T(8,128)} %shard_map.145) | data formatting | bytes 73728

commit v3 on v2

--- a/solution.py
+++ b/solution.py
@@ -17,6 +17,7 @@
 CORE = 384
 CHIPS = 8
 SIDE = TILE // 2
+LANES = 128
 FAR = (4, 3, 5, 2, 6, 1, 7)
 BLK = 16
 HALF = CHIPS * BLK
@@ -50,12 +51,14 @@
             for u, k in zip(rows, live)
         ]
     )
-    wtab = np.concatenate([np.cos(angles(pixel, freq[:SIDE])), -np.sin(angles(pixel, freq[:SIDE]))], 1) * scale
-    wtab[:, SIDE] = np.cos(angles(pixel, freq[SIDE : SIDE + 1]))[:, 0] * scale
+    cos, sin = np.cos(angles(pixel, freq[:SIDE])), -np.sin(angles(pixel, freq[:SIDE]))
+    sin[:, 0] = np.cos(angles(pixel, freq[SIDE : SIDE + 1]))[:, 0]
+    wtab = np.concatenate([cos[:, :LANES], sin[:, :LANES], cos[:, LANES:], sin[:, LANES:]], 1) * scale
     pgt = np.stack(
         [np.concatenate([np.cos(angles(u, offset)) * k, -np.sin(angles(u, offset)) * k]) for u, k in zip(rows, live)]
     )
-    order = np.concatenate([freq[:SIDE], freq[SIDE : SIDE + 1], freq[:SIDE:-1]])
+    minus = np.concatenate([freq[SIDE : SIDE + 1], freq[:SIDE:-1]])
+    order = np.concatenate([freq[:LANES], minus[:LANES], freq[LANES:SIDE], minus[LANES:]])
     cos, sin = np.cos(angles(offset, order)), np.sin(angles(offset, order))
     cos, sin = np.tile(cos, (4, 1)), np.tile(sin, (4, 1))
     pgw = np.block([[cos, -sin], [sin, cos]])
@@ -99,8 +102,8 @@
     ytab_h, xtab_h,
     out,
     foot, anchor, degree, powers, flux, variance, basis, pgt, taper, strip, otf_all, rowh, first, last, right, left, ap, ftab, wtab, pgw, ytab, xtab,
-    psf_own, psf_sib, psf_all, num_sib_out, num_sib_in, num_own, num_out, num_in, ex_in, ex_sum,
-    t_own, t_sib, part_out, part_in,
+    psf_own, psf_sib, psf_all, num_sib_out, num_sib_in, num_own, num_out, num_in, ex_out, ex_in, ex_sum,
+    t_own, t_sib, part_out,
     load_sem, halo_send, halo_recv, sib_send, sib_recv, psf_send, psf_recv, num_send, num_recv,
     ex_send, ex_recv, part_send, part_recv,
 ):
@@ -117,10 +120,15 @@
     def near(dr, dc):
         return {"trow": (r + dr + 4) % 4, "tcol": (c + dc + 4) % 4}
 
-    around = [(-1, -1), (-1, 1), (1, -1), (1, 1), (0, -1), (0, 1), (-1, 0), (1, 0)]
+    around = [(-1, -1), (-1, 1), (0, -1), (-1, 0), (1, 0), (0, 1), (1, -1), (1, 1)]
+    inside = [(r + dr >= 0) & (r + dr < 4) & (c + dc >= 0) & (c + dc < 4) for dr, dc in around]
     barrier = pltpu.get_barrier_semaphore()
-    for dr, dc in around:
-        pl.semaphore_signal(barrier, inc=1, device_id=near(dr, dc), device_id_type=MESH)
+    for at, there in zip(around, inside):
+
+        @pl.when(there)
+        def _():
+            pl.semaphore_signal(barrier, inc=1, device_id=near(*at), device_id_type=MESH)
+
     for k in FAR:
         pl.semaphore_signal(barrier, inc=1, device_id={"exp": along(k)}, device_id_type=MESH)
     pl.semaphore_signal(barrier, inc=1, device_id=sib, device_id_type=MESH)
@@ -138,34 +146,51 @@
         load.start()
         loads.append(load)
 
-    def remote(src, dst, send, recv, where):
-        copy = pltpu.make_async_remote_copy(
+    def describe(src, dst, send, recv, where):
+        return pltpu.make_async_remote_copy(
             src_ref=src, dst_ref=dst, send_sem=send, recv_sem=recv, device_id=where, device_id_type=MESH
         )
+
+    def remote(*args):
+        copy = describe(*args)
         copy.start()
         return copy
+
+    def others(first_chips):
+        place = jnp.where(z > 4, 2 * (z - 4) - 1, jnp.where(z == 0, CHIPS - 1, 2 * (4 - z))) if first_chips else z
+        for i in range(CHIPS - 1):
+            m = i + (i >= place).astype(jnp.int32)
+            chip = jnp.where(m % 2 == 1, 4 + (m + 1) // 2, 4 - m // 2) if first_chips else m
+            yield (chip - z + 2 * CHIPS) % CHIPS
 
     loads[0].wait()
     loads[1].wait()
     low = lax.broadcasted_iota(jnp.int32, (CORE, 128), 1) < HALO
     first[...] = jnp.where(low, strip[0, 0].astype(F32), pltpu.roll(strip[0, 1].astype(F32), HALO, 1)).astype(BF16)
     last[...] = jnp.where(low, pltpu.roll(strip[1, 0].astype(F32), HALO, 1), strip[1, 1].astype(F32)).astype(BF16)
-    pl.semaphore_wait(barrier, len(around) + CHIPS)
+    pl.semaphore_wait(barrier, sum(there.astype(jnp.int32) for there in inside) + CHIPS)
     top, low_rows = pl.ds(0, HALO), pl.ds(CORE - HALO, HALO)
     at_next, at_prev = pl.ds(CORE, HALO), pl.ds(CORE + HALO, HALO)
     pieces = [
         (first.at[top, :], right.at[at_next, :]),
         (last.at[top, :], left.at[at_next, :]),
+        (first, right.at[pl.ds(0, CORE), :]),
+        (stamps.at[:, top, :], rowh.at[:, pl.ds(0, HALO), :]),
+        (stamps.at[:, low_rows, :], rowh.at[:, pl.ds(HALO, HALO), :]),
+        (last, left.at[pl.ds(0, CORE), :]),
         (first.at[low_rows, :], right.at[at_prev, :]),
         (last.at[low_rows, :], left.at[at_prev, :]),
-        (first, right.at[pl.ds(0, CORE), :]),
-        (last, left.at[pl.ds(0, CORE), :]),
-        (stamps.at[:, top, :], rowh.at[:, pl.ds(0, HALO), :]),
-        (stamps.at[:, low_rows, :], rowh.at[:, pl.ds(HALO, HALO), :]),
     ]
     halos = [
-        remote(src, dst, halo_send.at[i], halo_recv.at[i], near(*around[i])) for i, (src, dst) in enumerate(pieces)
+        describe(src, dst, halo_send.at[i], halo_recv.at[i], near(*around[i])) for i, (src, dst) in enumerate(pieces)
     ]
+    for i in (0, 1, 6, 7, 2, 5, 3, 4):
+        pl.when(inside[i])(halos[i].start)
+    for i, (_, dst) in enumerate(pieces):
+
+        @pl.when(jnp.logical_not(inside[7 - i]))
+        def _():
+            dst[...] = jnp.zeros(dst.shape, BF16)
 
     for load in loads[2:9]:
         load.wait()
@@ -232,8 +257,8 @@
 
     for load in loads[11:15]:
         load.wait()
-    for copy in halos:
-        copy.wait_recv()
+    for i, copy in enumerate(halos):
+        pl.when(inside[7 - i])(copy.wait_recv)
     cover = []
     for e in range(2):
         cover.append(
@@ -261,22 +286,27 @@
         ap[e, CORE : CORE + HALO, CORE:TILE] = (corner[0:HALO] * (taper2[0:HALO] * up)).astype(BF16)
         ap[e, CORE + HALO : TILE, CORE:TILE] = (corner[HALO:] * (taper2[HALO:] * down)).astype(BF16)
 
-    lane0 = lax.broadcasted_iota(jnp.int32, (ROWS, SIDE), 1) == 0
-
-    def numerator(q, side):
+    lane0 = lax.broadcasted_iota(jnp.int32, (ROWS, LANES), 1) == 0
+
+    def halves(q):
+        return [dot(ftab[q], ap[e]).astype(BF16) for e in range(2)]
+
+    def numerator(half, side, chunk):
+        cols = slice(SIDE * chunk, SIDE * chunk + SIDE)
         total_re = total_im = None
         for e in range(2):
-            half = dot(ftab[q], ap[e]).astype(BF16)
-            prod = dot(half, wtab[...])
-            re_cos, re_sin = prod[:ROWS, :SIDE], prod[:ROWS, SIDE:]
-            im_cos, im_sin = prod[ROWS:, :SIDE], prod[ROWS:, SIDE:]
-            spec_re = jnp.concatenate(
-                [re_cos - jnp.where(lane0, 0.0, im_sin), jnp.where(lane0, re_sin, re_cos + im_sin)], axis=1
-            )
-            spec_im = jnp.concatenate(
-                [im_cos + jnp.where(lane0, 0.0, re_sin), jnp.where(lane0, im_sin, im_cos - re_sin)], axis=1
-            )
-            otf_re, otf_im = otf_all[side, e, :, :TILE], otf_all[side, e, :, TILE:]
+            prod = dot(half[e], wtab[:, cols])
+            re_cos, re_sin = prod[:ROWS, :LANES], prod[:ROWS, LANES:]
+            im_cos, im_sin = prod[ROWS:, :LANES], prod[ROWS:, LANES:]
+            if chunk == 0:
+                plus = [re_cos - jnp.where(lane0, 0.0, im_sin), im_cos + jnp.where(lane0, 0.0, re_sin)]
+                minus = [jnp.where(lane0, re_sin, re_cos + im_sin), jnp.where(lane0, im_sin, im_cos - re_sin)]
+            else:
+                plus = [re_cos - im_sin, im_cos + re_sin]
+                minus = [re_cos + im_sin, im_cos - re_sin]
+            spec_re, spec_im = (jnp.concatenate(pair, axis=1) for pair in zip(plus, minus))
+            otf_re = otf_all[side, e, :, cols]
+            otf_im = otf_all[side, e, :, TILE + SIDE * chunk : TILE + SIDE * chunk + SIDE]
             w = wnum[e][0:1, 0:1]
             part_re = w * (otf_re * spec_re + otf_im * spec_im)
             part_im = w * (otf_re * spec_im - otf_im * spec_re)
@@ -284,32 +314,40 @@
             total_im = part_im if e == 0 else total_im + part_im
         return total_re, total_im
 
-    num_re, num_im = numerator(1 - p, 0)
-    num_sib_out[0] = num_re.astype(BF16)
-    num_sib_out[1] = num_im.astype(BF16)
-    num_pair = remote(num_sib_out, num_sib_in, sib_send.at[1], sib_recv.at[1], sib)
-    num_re, num_im = numerator(p, 1)
-    num_pair.wait_recv()
-    num_re = num_re + num_sib_in[0].astype(F32)
-    num_im = num_im + num_sib_in[1].astype(F32)
-    num_own[0] = num_re
-    num_own[1] = num_im
-    num_out[0] = num_re.astype(BF16)
-    num_out[1] = num_im.astype(BF16)
-    num_copies = [
-        remote(
-            num_out.at[:, pl.ds(pl.multiple_of(BLK * ((z + k) % CHIPS), BLK), BLK), :],
-            num_in.at[k],
-            num_send.at[k],
-            num_recv.at[k],
+    def num_copy(chunk, k):
+        return describe(
+            num_out.at[chunk, :, pl.ds(pl.multiple_of(BLK * ((z + k) % CHIPS), BLK), BLK), :],
+            num_in.at[chunk, k],
+            num_send.at[chunk, k],
+            num_recv.at[chunk, k],
             {"exp": along(k)},
         )
-        for k in FAR
-    ]
+
+    half = halves(1 - p)
+    num_pairs = []
+    for chunk in range(2):
+        for i, part in enumerate(numerator(half, 0, chunk)):
+            num_sib_out[chunk, i] = part.astype(BF16)
+        num_pairs.append(
+            remote(num_sib_out.at[chunk], num_sib_in.at[chunk], sib_send.at[1 + chunk], sib_recv.at[1 + chunk], sib)
+        )
+    half = halves(p)
+    num_copies = []
+    for chunk in range(2):
+        parts = numerator(half, 1, chunk)
+        num_pairs[chunk].wait_recv()
+        for i, part in enumerate(parts):
+            part = part + num_sib_in[chunk, i].astype(F32)
+            num_own[i, :, SIDE * chunk : SIDE * chunk + SIDE] = part
+            num_out[chunk, i] = part[:HALF].astype(BF16)
+            ex_out[i, :, SIDE * chunk : SIDE * chunk + SIDE] = part[HALF:].astype(BF16)
+        for k in others(True):
+            num_copy(chunk, k).start()
+        num_copies += [num_copy(chunk, k) for k in FAR]
 
     def extra(at):
         return pltpu.make_async_remote_copy(
-            src_ref=num_out.at[:, pl.ds(HALF, BLK), :],
+            src_ref=ex_out,
             dst_ref=ex_in.at[at],
             send_sem=ex_send,
             recv_sem=ex_recv.at[at],
@@ -362,21 +400,26 @@
         ex_sum[...] = total
 
     sums = num_own[:, pl.ds(start, BLK), :]
-    for k, copy in reversed(list(zip(FAR, num_copies))):
-        copy.wait_recv()
-        sums = sums + num_in[k].astype(F32)
+    for i in reversed(range(len(FAR))):
+        num_copies[i].wait_recv()
+        num_copies[len(FAR) + i].wait_recv()
+        k = FAR[i]
+        sums = sums + jnp.concatenate([num_in[0, k], num_in[1, k]], axis=2).astype(F32)
     norm = lax.rsqrt(den + 1.0)
     s_re = jnp.concatenate([sums[0], ex_sum[0]], axis=0) * norm
     s_im = jnp.concatenate([sums[1], ex_sum[1]], axis=0) * norm
     loads[15].wait()
     loads[16].wait()
     lane0 = lax.broadcasted_iota(jnp.int32, (2 * BLK, SIDE), 1) == 0
-    (re_p, re_m), (im_p, im_m) = ((x[:, :SIDE], x[:, SIDE:]) for x in (s_re, s_im))
+    (re_p, re_m), (im_p, im_m) = (
+        [jnp.concatenate([x[:, at : at + LANES], x[:, SIDE + at : SIDE + at + LANES]], axis=1) for at in (0, LANES)]
+        for x in (s_re, s_im)
+    )
     top_rows = [jnp.where(lane0, re_p, re_p + re_m), jnp.where(lane0, re_m, im_m - im_p)]
     low_rows = [jnp.where(lane0, im_p, im_p + im_m), jnp.where(lane0, im_m, re_p - re_m)]
     folded = jnp.concatenate([jnp.concatenate(top_rows, axis=1), jnp.concatenate(low_rows, axis=1)], axis=0)
     t_own[...] = dot(folded.astype(BF16), ytab[...]).astype(BF16)
-    t_pair = remote(t_own, t_sib, sib_send.at[2], sib_recv.at[2], sib)
+    t_pair = remote(t_own, t_sib, sib_send.at[3], sib_recv.at[3], sib)
     image = dot(xtab[0], t_own[...])
     t_pair.wait_recv()
     image = image + dot(xtab[1], t_sib[...])
@@ -385,24 +428,33 @@
         part_out[t] = jnp.concatenate(
             [block[:, 128 * i : 128 * i + 128] for i in range(3)] + [jnp.zeros((PACK - 3 * OUT, 128), F32)], axis=0
         ).astype(BF16)
-    parts = [
-        remote(
-            part_out.at[(z + k) % CHIPS], part_in.at[k], part_send.at[k], part_recv.at[k], {"exp": along(k)}
-        )
-        for k in FAR
-    ]
-    total = part_out[z].astype(F32)
-    for k, copy in reversed(list(zip(FAR, parts))):
+    def part_copy(k):
+        return describe(
+            part_out.at[(z + k) % CHIPS], out.at[k], part_send.at[k], part_recv.at[k], {"exp": along(k)}
+        )
+
+    for k in others(False):
+        part_copy(k).start()
+    parts = [part_copy(k) for k in FAR]
+    mine = pltpu.make_async_copy(part_out.at[z], out.at[0], load_sem.at[0])
+    mine.start()
+    mine.wait()
+    for copy in parts:
         copy.wait_recv()
-        total = total + part_in[k].astype(F32)
-    for i in range(3):
-        out[0, :, 128 * i : 128 * i + 128] = total[OUT * i : OUT * (i + 1)]
-    for copy in halos + psf_copies + [psf_pair, num_pair, t_pair] + num_copies + parts:
+    for i, copy in enumerate(halos):
+        pl.when(inside[i])(copy.wait_send)
+    for copy in psf_copies + num_pairs + [psf_pair, t_pair] + num_copies + parts:
         copy.wait_send()
 
     @pl.when((p == 1) & (z < CHIPS - 1))
     def _():
         extra(z).wait_send()
+
+
+def finish(parts, out):
+    total = jnp.sum(parts[...].astype(F32), axis=0)
+    for i in range(3):
+        out[0, :, LANES * i : LANES * (i + 1)] = total[OUT * i : OUT * (i + 1)]
 
 
 def body(stamps, footprint, psf_anchor, psf_degree, psf_powers, psf_basis, flux, variance):
@@ -410,11 +462,11 @@
     vmem = pl.BlockSpec(memory_space=pltpu.VMEM)
     hbm = pl.BlockSpec(memory_space=pl.ANY)
     dma = pltpu.SemaphoreType.DMA
-    return pl.pallas_call(
+    parts = pl.pallas_call(
         kernel,
-        out_shape=jax.ShapeDtypeStruct((1, OUT, CORE), F32),
+        out_shape=jax.ShapeDtypeStruct((CHIPS, PACK, 128), BF16),
         in_specs=[hbm] * 15,
-        out_specs=vmem,
+        out_specs=hbm,
         scratch_shapes=[
             pltpu.SMEM((2, 4), jnp.int32),
             pltpu.SMEM((2, 2), jnp.int32),
@@ -441,26 +493,26 @@
             pltpu.VMEM((PS + BLK, 128), BF16),
             pltpu.VMEM((PS + BLK, 128), BF16),
             pltpu.VMEM((CHIPS, PS + BLK, 128), BF16),
-            pltpu.VMEM((2, ROWS, TILE), BF16),
-            pltpu.VMEM((2, ROWS, TILE), BF16),
+            pltpu.VMEM((2, 2, ROWS, SIDE), BF16),
+            pltpu.VMEM((2, 2, ROWS, SIDE), BF16),
             pltpu.VMEM((2, ROWS, TILE), F32),
-            pltpu.VMEM((2, ROWS, TILE), BF16),
-            pltpu.VMEM((CHIPS, 2, BLK, TILE), BF16),
+            pltpu.VMEM((2, 2, HALF, SIDE), BF16),
+            pltpu.VMEM((2, CHIPS, 2, BLK, SIDE), BF16),
+            pltpu.VMEM((2, BLK, TILE), BF16),
             pltpu.VMEM((CHIPS - 1, 2, BLK, TILE), BF16),
             pltpu.VMEM((2, BLK, TILE), F32),
             pltpu.VMEM((4 * BLK, CORE), BF16),
             pltpu.VMEM((4 * BLK, CORE), BF16),
             pltpu.VMEM((CHIPS, PACK, 128), BF16),
-            pltpu.VMEM((CHIPS, PACK, 128), BF16),
             dma((17,)),
             dma((8,)),
             dma((8,)),
-            dma((3,)),
-            dma((3,)),
+            dma((4,)),
+            dma((4,)),
             dma((CHIPS,)),
             dma((CHIPS,)),
-            dma((CHIPS,)),
-            dma((CHIPS,)),
+            dma((2, CHIPS)),
+            dma((2, CHIPS)),
             dma,
             dma((CHIPS - 1,)),
             dma((CHIPS,)),
@@ -474,6 +526,9 @@
         psf_basis.transpose(1, 0, 2), pgt, taper,
         stamps, ftab, wtab, pgw, ytab, xtab,
     )
+    return pl.pallas_call(
+        finish, out_shape=jax.ShapeDtypeStruct((1, OUT, CORE), F32), in_specs=[vmem], out_specs=vmem
+    )(parts)
 
 
 def solution(mesh):

time: 36.4 us -> 32.9 us (0.904)
  Pallas kernels: 34.8 us -> 32.6 us
  local copies, waits for them, and re-layouts: 1.39 us -> 0 us
    pallas_call x1 -> x2, Pallas kernels: 34.8 us -> 32.6 us  [the longest x1 31.1 us: body(): pl.pallas_call(kernel, out_shape=jax.ShapeDtypeStruct((CHIPS, PACK, 128),...]
    unnamed x1 -> x0, local copies, waits for them, and re-layouts: 1.39 us -> none
where the time goes in v3:
time: 32.9 us; the launch traced here: 32.6 us
  Pallas kernels  32.6 us (99%)
    pallas_call x1, Pallas kernels, body(): pl.pallas_call(kernel, out_shape=jax.ShapeDtypeStruct((CHIPS, PACK, 128),...  31.1 us
    pallas_call x1, Pallas kernels, body(): pl.pallas_call(finish, out_shape=jax.ShapeDtypeStruct((1, OUT, CORE), F32...  1.56 us

profile of v3, /device:TPU:1, one launch (start us, length us, event | category | flops | bytes accessed | tf_op | source)
XLA Modules:
  0.0 32.6 jit_solution(5306979063374992922)
XLA Ops:
  0.0 31.1 %shard_map.145.parts = bf16[8,80,128]{2,1,0:T(8,128)(2,1)} custom-call(s32[2,4]{1,0:T(2,128)} %foot_h.1, s32[2,2]{1,0:T(2,128)} %anchor_h.1, s32[2]{0:T(128)} %degree_h.1, s32[2,2,10]{2,1,0:T(2,128)} %bitcast.3, f32[2]{0:T(128)} %flux_h.1, f32[2]{0:T(128)} %variance_h.1, f32[10,2,1024]{2,1,0:T(2,128)} %bitcast.2, bf16[2,288,32]{2,1,0:T(8,128)(2,1)} %constant.16.clone.pgt_h, ...), custom_call_target="tpu_custom_call" | custom-call | tf_op jit(solution)/shard_map/pallas_call | solution.py:465
  31.1 1.6 %shard_map.146 = f32[1,24,384]{2,1,0:T(8,128)} custom-call(bf16[8,80,128]{2,1,0:T(8,128)(2,1)} %shard_map.145.parts), custom_call_target="tpu_custom_call" | custom-call | tf_op jit(solution)/shard_map/pallas_call | solution.py:529

commit v4 on v3

--- a/solution.py
+++ b/solution.py
@@ -19,6 +19,8 @@
 SIDE = TILE // 2
 LANES = 128
 FAR = (4, 3, 5, 2, 6, 1, 7)
+NUM_ORDER = (3, 2, 1, 4, 0, 5, 6, 7)
+PART_ORDER = (0, 1, 2, 3, 4, 5, 6, 7)
 BLK = 16
 HALF = CHIPS * BLK
 ROWS = HALF + BLK
@@ -101,11 +103,12 @@
     foot_h, anchor_h, degree_h, powers_h, flux_h, variance_h, basis_h, pgt_h, taper_h, stamps, ftab_h, wtab_h, pgw_h,
     ytab_h, xtab_h,
     out,
-    foot, anchor, degree, powers, flux, variance, basis, pgt, taper, strip, otf_all, rowh, first, last, right, left, ap, ftab, wtab, pgw, ytab, xtab,
+    foot, anchor, degree, powers, flux, variance, basis, pgt, taper, strip, otf_all, num_first, rowh, cols, cols_in, corners,
+    corners_in, ap, ftab, wtab, pgw, ytab, xtab,
     psf_own, psf_sib, psf_all, num_sib_out, num_sib_in, num_own, num_out, num_in, ex_out, ex_in, ex_sum,
     t_own, t_sib, part_out,
     load_sem, halo_send, halo_recv, sib_send, sib_recv, psf_send, psf_recv, num_send, num_recv,
-    ex_send, ex_recv, part_send, part_recv,
+    ex_send, ex_recv, part_send, part_recv, ready,
 ):
     group = lax.axis_index("exp")
     r = lax.axis_index("trow")
@@ -130,7 +133,11 @@
             pl.semaphore_signal(barrier, inc=1, device_id=near(*at), device_id_type=MESH)
 
     for k in FAR:
-        pl.semaphore_signal(barrier, inc=1, device_id={"exp": along(k)}, device_id_type=MESH)
+
+        @pl.when((z + k) % CHIPS > z)
+        def _():
+            pl.semaphore_signal(barrier, inc=1, device_id={"exp": along(k)}, device_id_type=MESH)
+
     pl.semaphore_signal(barrier, inc=1, device_id=sib, device_id_type=MESH)
     loads = []
     for i, (src, dst) in enumerate(
@@ -156,37 +163,47 @@
         copy.start()
         return copy
 
-    def others(first_chips):
-        place = jnp.where(z > 4, 2 * (z - 4) - 1, jnp.where(z == 0, CHIPS - 1, 2 * (4 - z))) if first_chips else z
-        for i in range(CHIPS - 1):
-            m = i + (i >= place).astype(jnp.int32)
-            chip = jnp.where(m % 2 == 1, 4 + (m + 1) // 2, 4 - m // 2) if first_chips else m
-            yield (chip - z + 2 * CHIPS) % CHIPS
+    def to_others(chips, copy):
+        for chip in chips:
+            pl.when(z != chip)(lambda chip=chip: copy((chip - z + CHIPS) % CHIPS).start())
 
     loads[0].wait()
     loads[1].wait()
-    low = lax.broadcasted_iota(jnp.int32, (CORE, 128), 1) < HALO
-    first[...] = jnp.where(low, strip[0, 0].astype(F32), pltpu.roll(strip[0, 1].astype(F32), HALO, 1)).astype(BF16)
-    last[...] = jnp.where(low, pltpu.roll(strip[1, 0].astype(F32), HALO, 1), strip[1, 1].astype(F32)).astype(BF16)
-    pl.semaphore_wait(barrier, sum(there.astype(jnp.int32) for there in inside) + CHIPS)
-    top, low_rows = pl.ds(0, HALO), pl.ds(CORE - HALO, HALO)
-    at_next, at_prev = pl.ds(CORE, HALO), pl.ds(CORE + HALO, HALO)
+    low = lax.broadcasted_iota(jnp.int32, (CORE // 2, 128), 1) < HALO
+    turned = [[pltpu.roll(strip[side, e].astype(F32), HALO, 1) for e in range(2)] for side in range(2)]
+    for e in range(2):
+        cols[0, e] = jnp.where(low, strip[0, e, : CORE // 2].astype(F32), turned[0][e][CORE // 2 :]).astype(BF16)
+        cols[1, e] = jnp.where(low, turned[1][e][: CORE // 2], strip[1, e, CORE // 2 :].astype(F32)).astype(BF16)
+    for i, rows in enumerate((slice(0, HALO), slice(CORE - HALO, CORE))):
+        corners[i, 0] = jnp.where(low[:HALO], strip[0, 0, rows].astype(F32), turned[0][1][rows]).astype(BF16)
+        corners[i, 1] = jnp.where(low[:HALO], turned[1][0][rows], strip[1, 1, rows].astype(F32)).astype(BF16)
+    pl.semaphore_wait(barrier, sum(there.astype(jnp.int32) for there in inside) + 1 + z)
     pieces = [
-        (first.at[top, :], right.at[at_next, :]),
-        (last.at[top, :], left.at[at_next, :]),
-        (first, right.at[pl.ds(0, CORE), :]),
-        (stamps.at[:, top, :], rowh.at[:, pl.ds(0, HALO), :]),
-        (stamps.at[:, low_rows, :], rowh.at[:, pl.ds(HALO, HALO), :]),
-        (last, left.at[pl.ds(0, CORE), :]),
-        (first.at[low_rows, :], right.at[at_prev, :]),
-        (last.at[low_rows, :], left.at[at_prev, :]),
+        (0, corners.at[0, 0], corners_in.at[0, 0]),
+        (1, corners.at[0, 1], corners_in.at[0, 1]),
+        (6, corners.at[1, 0], corners_in.at[1, 0]),
+        (7, corners.at[1, 1], corners_in.at[1, 1]),
     ]
+    for e in range(2):
+        pieces += [
+            (2, cols.at[0, e], cols_in.at[0, e]),
+            (5, cols.at[1, e], cols_in.at[1, e]),
+            (3, stamps.at[e, pl.ds(0, HALO), :], rowh.at[e, pl.ds(0, HALO), :]),
+            (4, stamps.at[e, pl.ds(CORE - HALO, HALO), :], rowh.at[e, pl.ds(HALO, HALO), :]),
+        ]
     halos = [
-        describe(src, dst, halo_send.at[i], halo_recv.at[i], near(*around[i])) for i, (src, dst) in enumerate(pieces)
+        (i, describe(src, dst, halo_send.at[n], halo_recv.at[n], near(*around[i])))
+        for n, (i, src, dst) in enumerate(pieces)
     ]
-    for i in (0, 1, 6, 7, 2, 5, 3, 4):
-        pl.when(inside[i])(halos[i].start)
-    for i, (_, dst) in enumerate(pieces):
+    for i, copy in halos:
+        pl.when(inside[i])(copy.start)
+    for k in FAR:
+
+        @pl.when((z + k) % CHIPS < z)
+        def _():
+            pl.semaphore_signal(ready.at[CHIPS - k], inc=1, device_id={"exp": along(k)}, device_id_type=MESH)
+
+    for i, _, dst in pieces:
 
         @pl.when(jnp.logical_not(inside[7 - i]))
         def _():
@@ -248,71 +265,59 @@
         for e in range(2):
             one = jnp.where(lane_r == 2 * p + e, lift, 0.0).astype(BF16)
             otf_all[side, e] = dot(jnp.concatenate([one[:ROWS], one[ROWS:]], axis=1), pgw[...])
-        if side == 0:
-            psf_pair.wait_recv()
-            psf_all[0] = (psf_own[...].astype(F32) + psf_sib[...].astype(F32)).astype(BF16)
-            psf_copies = [
-                remote(psf_all.at[0], psf_all.at[k], psf_send.at[k], psf_recv.at[k], {"exp": along(k)}) for k in FAR
-            ]
 
     for load in loads[11:15]:
         load.wait()
-    for i, copy in enumerate(halos):
-        pl.when(inside[7 - i])(copy.wait_recv)
-    cover = []
-    for e in range(2):
-        cover.append(
-            [
-                jnp.where((foot[e, lo] <= at) & (at < foot[e, lo + 1]), 1.0, 0.0)
-                for lo, at in ((0, r + 1), (0, r - 1), (2, c + 1), (2, c - 1))
-            ]
-        )
-    lane_s = lax.broadcasted_iota(jnp.int32, (TILE, 128), 1) < HALO
+    lane_s = lax.broadcasted_iota(jnp.int32, (CORE, 128), 1) < HALO
     line_r = taper[0]
     line_c = taper[1]
-    right_v, left_v = right[...].astype(F32), left[...].astype(F32)
-    right_t, left_t = pltpu.roll(right_v, HALO, 1), pltpu.roll(left_v, HALO, 1)
-    for e in range(2):
-        up, down, after, before = cover[e]
-        wide = jnp.concatenate([line_r] * 3, axis=1)
+    wide = jnp.concatenate([line_r] * 3, axis=1)
+
+    def apodize(e):
+        for i, copy in halos[4 + 4 * e : 8 + 4 * e]:
+            pl.when(inside[7 - i])(copy.wait_recv)
+        up, down, after, before = [
+            jnp.where((foot[e, lo] <= at) & (at < foot[e, lo + 1]), 1.0, 0.0)
+            for lo, at in ((0, r + 1), (0, r - 1), (2, c + 1), (2, c - 1))
+        ]
         ap[e, CORE : CORE + HALO, 0:CORE] = (rowh[e, 0:HALO, :].astype(F32) * (wide[0:HALO] * up)).astype(BF16)
         ap[e, CORE + HALO : TILE, 0:CORE] = (rowh[e, HALO:, :].astype(F32) * (wide[HALO:] * down)).astype(BF16)
-        side = jnp.where(lane_s, right_v, left_t) if e == 0 else jnp.where(lane_s, right_t, left_v)
-        keep = jnp.where(lane_s[0:128], after, before) * line_c
-        for t in range(3):
-            ap[e, 128 * t : 128 * t + 128, CORE:TILE] = (side[128 * t : 128 * t + 128] * keep).astype(BF16)
-        corner = side[CORE:TILE]
-        taper2 = line_r * line_c * jnp.where(lane_s[0:128], after, before)
-        ap[e, CORE : CORE + HALO, CORE:TILE] = (corner[0:HALO] * (taper2[0:HALO] * up)).astype(BF16)
-        ap[e, CORE + HALO : TILE, CORE:TILE] = (corner[HALO:] * (taper2[HALO:] * down)).astype(BF16)
+        right, left = cols_in[0, e].astype(F32), cols_in[1, e].astype(F32)
+        side = jnp.concatenate(
+            [jnp.where(low, right, pltpu.roll(left, HALO, 1)), jnp.where(low, pltpu.roll(right, HALO, 1), left)], axis=0
+        )
+        keep = jnp.where(lane_s, after, before)
+        ap[e, 0:CORE, CORE:TILE] = (side * (jnp.concatenate([line_c] * 3, axis=0) * keep)).astype(BF16)
+        for i, rows in enumerate((slice(0, HALO), slice(HALO, 2 * HALO))):
+            right, left = corners_in[i, 0].astype(F32), corners_in[i, 1].astype(F32)
+            if e == 0:
+                corner = jnp.where(low[:HALO], right, pltpu.roll(left, HALO, 1))
+            else:
+                corner = jnp.where(low[:HALO], pltpu.roll(right, HALO, 1), left)
+            taper2 = line_r[rows] * line_c[rows] * keep[:HALO] * (up if i == 0 else down)
+            ap[e, CORE + HALO * i : CORE + HALO * (i + 1), CORE:TILE] = (corner * taper2).astype(BF16)
 
     lane0 = lax.broadcasted_iota(jnp.int32, (ROWS, LANES), 1) == 0
 
-    def halves(q):
-        return [dot(ftab[q], ap[e]).astype(BF16) for e in range(2)]
-
-    def numerator(half, side, chunk):
+    def halved(q, e):
+        return dot(ftab[q], ap[e]).astype(BF16)
+
+    def numerator(half, side, chunk, e):
         cols = slice(SIDE * chunk, SIDE * chunk + SIDE)
-        total_re = total_im = None
-        for e in range(2):
-            prod = dot(half[e], wtab[:, cols])
-            re_cos, re_sin = prod[:ROWS, :LANES], prod[:ROWS, LANES:]
-            im_cos, im_sin = prod[ROWS:, :LANES], prod[ROWS:, LANES:]
-            if chunk == 0:
-                plus = [re_cos - jnp.where(lane0, 0.0, im_sin), im_cos + jnp.where(lane0, 0.0, re_sin)]
-                minus = [jnp.where(lane0, re_sin, re_cos + im_sin), jnp.where(lane0, im_sin, im_cos - re_sin)]
-            else:
-                plus = [re_cos - im_sin, im_cos + re_sin]
-                minus = [re_cos + im_sin, im_cos - re_sin]
-            spec_re, spec_im = (jnp.concatenate(pair, axis=1) for pair in zip(plus, minus))
-            otf_re = otf_all[side, e, :, cols]
-            otf_im = otf_all[side, e, :, TILE + SIDE * chunk : TILE + SIDE * chunk + SIDE]
-            w = wnum[e][0:1, 0:1]
-            part_re = w * (otf_re * spec_re + otf_im * spec_im)
-            part_im = w * (otf_re * spec_im - otf_im * spec_re)
-            total_re = part_re if e == 0 else total_re + part_re
-            total_im = part_im if e == 0 else total_im + part_im
-        return total_re, total_im
+        prod = dot(half, wtab[:, cols])
+        re_cos, re_sin = prod[:ROWS, :LANES], prod[:ROWS, LANES:]
+        im_cos, im_sin = prod[ROWS:, :LANES], prod[ROWS:, LANES:]
+        if chunk == 0:
+            plus = [re_cos - jnp.where(lane0, 0.0, im_sin), im_cos + jnp.where(lane0, 0.0, re_sin)]
+            minus = [jnp.where(lane0, re_sin, re_cos + im_sin), jnp.where(lane0, im_sin, im_cos - re_sin)]
+        else:
+            plus = [re_cos - im_sin, im_cos + re_sin]
+            minus = [re_cos + im_sin, im_cos - re_sin]
+        spec_re, spec_im = (jnp.concatenate(pair, axis=1) for pair in zip(plus, minus))
+        otf_re = otf_all[side, e, :, cols]
+        otf_im = otf_all[side, e, :, TILE + SIDE * chunk : TILE + SIDE * chunk + SIDE]
+        w = wnum[e][0:1, 0:1]
+        return w * (otf_re * spec_re + otf_im * spec_im), w * (otf_re * spec_im - otf_im * spec_re)
 
     def num_copy(chunk, k):
         return describe(
@@ -323,26 +328,47 @@
             {"exp": along(k)},
         )
 
-    half = halves(1 - p)
+    psf_pair.wait_recv()
+    psf_all[0] = (psf_own[...].astype(F32) + psf_sib[...].astype(F32)).astype(BF16)
+    psf_copies = [
+        describe(psf_all.at[0], psf_all.at[k], psf_send.at[k], psf_recv.at[k], {"exp": along(k)}) for k in FAR
+    ]
+    for k, copy in zip(FAR, psf_copies):
+        pl.when((z + k) % CHIPS < z)(copy.start)
+    for i, copy in halos[:4]:
+        pl.when(inside[7 - i])(copy.wait_recv)
+    apodize(0)
+    half = halved(1 - p, 0)
+    for chunk in range(2):
+        for i, part in enumerate(numerator(half, 0, chunk, 0)):
+            num_first[chunk, i] = part
+    apodize(1)
+    half = halved(1 - p, 1)
     num_pairs = []
     for chunk in range(2):
-        for i, part in enumerate(numerator(half, 0, chunk)):
-            num_sib_out[chunk, i] = part.astype(BF16)
+        for i, part in enumerate(numerator(half, 0, chunk, 1)):
+            num_sib_out[chunk, i] = (num_first[chunk, i] + part).astype(BF16)
         num_pairs.append(
             remote(num_sib_out.at[chunk], num_sib_in.at[chunk], sib_send.at[1 + chunk], sib_recv.at[1 + chunk], sib)
         )
-    half = halves(p)
+    for k, copy in zip(FAR, psf_copies):
+
+        @pl.when((z + k) % CHIPS > z)
+        def _():
+            pl.semaphore_wait(ready.at[k], 1)
+            copy.start()
+
+    half = [halved(p, e) for e in range(2)]
     num_copies = []
     for chunk in range(2):
-        parts = numerator(half, 1, chunk)
+        parts = [a + b for a, b in zip(*(numerator(half[e], 1, chunk, e) for e in range(2)))]
         num_pairs[chunk].wait_recv()
         for i, part in enumerate(parts):
             part = part + num_sib_in[chunk, i].astype(F32)
             num_own[i, :, SIDE * chunk : SIDE * chunk + SIDE] = part
             num_out[chunk, i] = part[:HALF].astype(BF16)
             ex_out[i, :, SIDE * chunk : SIDE * chunk + SIDE] = part[HALF:].astype(BF16)
-        for k in others(True):
-            num_copy(chunk, k).start()
+        to_others(NUM_ORDER, functools.partial(num_copy, chunk))
         num_copies += [num_copy(chunk, k) for k in FAR]
 
     def extra(at):
@@ -433,15 +459,14 @@
             part_out.at[(z + k) % CHIPS], out.at[k], part_send.at[k], part_recv.at[k], {"exp": along(k)}
         )
 
-    for k in others(False):
-        part_copy(k).start()
+    to_others(PART_ORDER, part_copy)
     parts = [part_copy(k) for k in FAR]
     mine = pltpu.make_async_copy(part_out.at[z], out.at[0], load_sem.at[0])
     mine.start()
     mine.wait()
     for copy in parts:
         copy.wait_recv()
-    for i, copy in enumerate(halos):
+    for i, copy in halos:
         pl.when(inside[i])(copy.wait_send)
     for copy in psf_copies + num_pairs + [psf_pair, t_pair] + num_copies + parts:
         copy.wait_send()
@@ -464,7 +489,7 @@
     dma = pltpu.SemaphoreType.DMA
     parts = pl.pallas_call(
         kernel,
-        out_shape=jax.ShapeDtypeStruct((CHIPS, PACK, 128), BF16),
+        out_shape=pltpu.VMEM((CHIPS, PACK, 128), BF16),
         in_specs=[hbm] * 15,
         out_specs=hbm,
         scratch_shapes=[
@@ -479,11 +504,12 @@
             pltpu.VMEM(taper.shape, F32),
             pltpu.VMEM((2, 2, CORE, 128), BF16),
             pltpu.VMEM((2, 2, ROWS, 2 * TILE), F32),
+            pltpu.VMEM((2, 2, ROWS, SIDE), F32),
             pltpu.VMEM((2, 2 * HALO, CORE), BF16),
-            pltpu.VMEM((CORE, 128), BF16),
-            pltpu.VMEM((CORE, 128), BF16),
-            pltpu.VMEM((TILE, 128), BF16),
-            pltpu.VMEM((TILE, 128), BF16),
+            pltpu.VMEM((2, 2, CORE // 2, 128), BF16),
+            pltpu.VMEM((2, 2, CORE // 2, 128), BF16),
+            pltpu.VMEM((2, 2, HALO, 128), BF16),
+            pltpu.VMEM((2, 2, HALO, 128), BF16),
             pltpu.VMEM((2, TILE, TILE), BF16),
             pltpu.VMEM(ftab.shape, BF16),
             pltpu.VMEM(wtab.shape, BF16),
@@ -505,8 +531,8 @@
             pltpu.VMEM((4 * BLK, CORE), BF16),
             pltpu.VMEM((CHIPS, PACK, 128), BF16),
             dma((17,)),
-            dma((8,)),
-            dma((8,)),
+            dma((12,)),
+            dma((12,)),
             dma((4,)),
             dma((4,)),
             dma((CHIPS,)),
@@ -517,15 +543,17 @@
             dma((CHIPS - 1,)),
             dma((CHIPS,)),
             dma((CHIPS,)),
+            pltpu.SemaphoreType.REGULAR((CHIPS,)),
         ],
         compiler_params=pltpu.CompilerParams(
-            collective_id=0, has_side_effects=True, vmem_limit_bytes=64 * 1024 * 1024 - 65536
+            collective_id=0, has_side_effects=True, vmem_limit_bytes=64 * 1024 * 1024 - 512 * 1024
         ),
     )(
         footprint, psf_anchor, psf_degree, psf_powers.transpose(0, 2, 1), flux, variance,
         psf_basis.transpose(1, 0, 2), pgt, taper,
         stamps, ftab, wtab, pgw, ytab, xtab,
     )
+    parts = pltpu.with_memory_space_constraint(parts, pltpu.VMEM)
     return pl.pallas_call(
         finish, out_shape=jax.ShapeDtypeStruct((1, OUT, CORE), F32), in_specs=[vmem], out_specs=vmem
     )(parts)

time: 32.9 us -> 31.1 us (0.945)
  Pallas kernels: 32.6 us -> 31.1 us
    pallas_call x1, Pallas kernels: 1.56 us -> 0.64 us  [body(): pl.pallas_call(finish, out_shape=jax.ShapeDtypeStruct((1, OUT, CORE), F32...]
    pallas_call x1, Pallas kernels: 31.1 us -> 30.4 us  [body(): pl.pallas_call(kernel, out_shape=pltpu.VMEM((CHIPS, PACK, 128), BF16), in...]
where the time goes in v4:
time: 31.1 us
  Pallas kernels  31.1 us (100%)
    pallas_call x1, Pallas kernels, body(): pl.pallas_call(kernel, out_shape=pltpu.VMEM((CHIPS, PACK, 128), BF16), in...  30.4 us
    pallas_call x1, Pallas kernels, body(): pl.pallas_call(finish, out_shape=jax.ShapeDtypeStruct((1, OUT, CORE), F32...  0.64 us

profile of v4, /device:TPU:1, one launch (start us, length us, event | category | flops | bytes accessed | tf_op | source)
XLA Modules:
  0.0 31.1 jit_solution(11143343260829621036)
XLA Ops:
  0.0 30.4 %shard_map.145.parts = bf16[8,80,128]{2,1,0:T(8,128)(2,1)S(1)} custom-call(s32[2,4]{1,0:T(2,128)} %foot_h.1, s32[2,2]{1,0:T(2,128)} %anchor_h.1, s32[2]{0:T(128)} %degree_h.1, s32[2,2,10]{2,1,0:T(2,128)} %bitcast.3, f32[2]{0:T(128)} %flux_h.1, f32[2]{0:T(128)} %variance_h.1, f32[10,2,1024]{2,1,0:T(2,128)} %bitcast.2, ...), custom_call_target="tpu_custom_call" | custom-call | tf_op jit(solution)/shard_map/pallas_call | solution.py:490
  30.4 0.6 %shard_map.146 = f32[1,24,384]{2,1,0:T(8,128)} custom-call(bf16[8,80,128]{2,1,0:T(8,128)(2,1)S(1)} %shard_map.145.parts), custom_call_target="tpu_custom_call" | custom-call | tf_op jit(solution)/shard_map/pallas_call | solution.py:557

commit v5 on v4

--- a/solution.py
+++ b/solution.py
@@ -65,8 +65,9 @@
     cos, sin = np.tile(cos, (4, 1)), np.tile(sin, (4, 1))
     pgw = np.block([[cos, -sin], [sin, cos]])
     core = np.arange(CORE) + HALO
-    ytab = np.concatenate([np.cos(angles(freq[:SIDE], core)), np.sin(angles(freq[:SIDE], core))]) * scale
-    ytab[SIDE] = np.cos(angles(freq[SIDE : SIDE + 1], core))[0] * scale
+    cos, sin = np.cos(angles(freq[:SIDE], core)), np.sin(angles(freq[:SIDE], core))
+    sin[0] = np.cos(angles(freq[SIDE : SIDE + 1], core))[0]
+    ytab = np.concatenate([cos[:LANES], sin[:LANES], cos[LANES:], sin[LANES:]]) * scale
     xtab = np.zeros((2 * CHIPS, 2, CHIPS * OUT, 4 * BLK))
     for z in range(CHIPS):
         for p in range(2):
@@ -360,6 +361,8 @@
 
     half = [halved(p, e) for e in range(2)]
     num_copies = []
+    row8 = lax.broadcasted_iota(jnp.int32, (8, LANES), 0)
+    nyquist = jnp.zeros((8, LANES), F32)
     for chunk in range(2):
         parts = [a + b for a, b in zip(*(numerator(half[e], 1, chunk, e) for e in range(2)))]
         num_pairs[chunk].wait_recv()
@@ -367,7 +370,12 @@
             part = part + num_sib_in[chunk, i].astype(F32)
             num_own[i, :, SIDE * chunk : SIDE * chunk + SIDE] = part
             num_out[chunk, i] = part[:HALF].astype(BF16)
-            ex_out[i, :, SIDE * chunk : SIDE * chunk + SIDE] = part[HALF:].astype(BF16)
+            for j in range(2):
+                nyquist = jnp.where(
+                    row8 == 4 * i + 2 * chunk + j,
+                    jnp.broadcast_to(part[HALF : HALF + 1, LANES * j : LANES * (j + 1)], row8.shape),
+                    nyquist,
+                )
         to_others(NUM_ORDER, functools.partial(num_copy, chunk))
         num_copies += [num_copy(chunk, k) for k in FAR]
 
@@ -380,6 +388,8 @@
             device_id={"exp": 2 * CHIPS - 1},
             device_id_type=MESH,
         )
+
+    ex_out[...] = jnp.concatenate([nyquist, jnp.zeros_like(nyquist)], axis=0).astype(BF16)
 
     @pl.when((p == 1) & (z < CHIPS - 1))
     def _():
@@ -420,31 +430,33 @@
     def _():
         for t in range(CHIPS - 1):
             extra(t).wait_recv()
-        total = num_own[:, HALF:ROWS, :]
+        total = nyquist
         for t in range(CHIPS - 1):
-            total = total + ex_in[t].astype(F32)
-        ex_sum[...] = total
-
-    sums = num_own[:, pl.ds(start, BLK), :]
-    for i in reversed(range(len(FAR))):
-        num_copies[i].wait_recv()
-        num_copies[len(FAR) + i].wait_recv()
-        k = FAR[i]
-        sums = sums + jnp.concatenate([num_in[0, k], num_in[1, k]], axis=2).astype(F32)
+            total = total + ex_in[t].astype(F32)[:8]
+        for i in range(8):
+            ex_sum[i // 4, 0:1, LANES * (i % 4) : LANES * (i % 4 + 1)] = total[i : i + 1]
+
     norm = lax.rsqrt(den + 1.0)
-    s_re = jnp.concatenate([sums[0], ex_sum[0]], axis=0) * norm
-    s_im = jnp.concatenate([sums[1], ex_sum[1]], axis=0) * norm
     loads[15].wait()
     loads[16].wait()
-    lane0 = lax.broadcasted_iota(jnp.int32, (2 * BLK, SIDE), 1) == 0
-    (re_p, re_m), (im_p, im_m) = (
-        [jnp.concatenate([x[:, at : at + LANES], x[:, SIDE + at : SIDE + at + LANES]], axis=1) for at in (0, LANES)]
-        for x in (s_re, s_im)
-    )
-    top_rows = [jnp.where(lane0, re_p, re_p + re_m), jnp.where(lane0, re_m, im_m - im_p)]
-    low_rows = [jnp.where(lane0, im_p, im_p + im_m), jnp.where(lane0, im_m, re_p - re_m)]
-    folded = jnp.concatenate([jnp.concatenate(top_rows, axis=1), jnp.concatenate(low_rows, axis=1)], axis=0)
-    t_own[...] = dot(folded.astype(BF16), ytab[...]).astype(BF16)
+    lane0 = lax.broadcasted_iota(jnp.int32, (2 * BLK, LANES), 1) == 0
+    t_all = None
+    for chunk in range(2):
+        cols = slice(SIDE * chunk, SIDE * chunk + SIDE)
+        sums = num_own[:, pl.ds(start, BLK), cols]
+        for k, copy in zip(FAR, num_copies[len(FAR) * chunk :]):
+            copy.wait_recv()
+            sums = sums + num_in[chunk, k].astype(F32)
+        s_re, s_im = (jnp.concatenate([sums[i], ex_sum[i, :, cols]], axis=0) * norm[:, cols] for i in range(2))
+        (re_p, re_m), (im_p, im_m) = ((x[:, :LANES], x[:, LANES:]) for x in (s_re, s_im))
+        even, odd = [re_p + re_m, im_p + im_m], [im_m - im_p, re_p - re_m]
+        if chunk == 0:
+            even = [jnp.where(lane0, a, b) for a, b in zip((re_p, im_p), even)]
+            odd = [jnp.where(lane0, a, b) for a, b in zip((re_m, im_m), odd)]
+        folded = jnp.concatenate([jnp.concatenate(pair, axis=1) for pair in zip(even, odd)], axis=0)
+        part = dot(folded.astype(BF16), ytab[cols, :])
+        t_all = part if chunk == 0 else t_all + part
+    t_own[...] = t_all.astype(BF16)
     t_pair = remote(t_own, t_sib, sib_send.at[3], sib_recv.at[3], sib)
     image = dot(xtab[0], t_own[...])
     t_pair.wait_recv()
@@ -524,8 +536,8 @@
             pltpu.VMEM((2, ROWS, TILE), F32),
             pltpu.VMEM((2, 2, HALF, SIDE), BF16),
             pltpu.VMEM((2, CHIPS, 2, BLK, SIDE), BF16),
-            pltpu.VMEM((2, BLK, TILE), BF16),
-            pltpu.VMEM((CHIPS - 1, 2, BLK, TILE), BF16),
+            pltpu.VMEM((BLK, LANES), BF16),
+            pltpu.VMEM((CHIPS - 1, BLK, LANES), BF16),
             pltpu.VMEM((2, BLK, TILE), F32),
             pltpu.VMEM((4 * BLK, CORE), BF16),
             pltpu.VMEM((4 * BLK, CORE), BF16),

time: 31.1 us -> 30.6 us (0.984)
  Pallas kernels: 31.1 us -> 30.5 us
    pallas_call x1, Pallas kernels: 30.4 us -> 29.9 us  [body(): pl.pallas_call(kernel, out_shape=pltpu.VMEM((CHIPS, PACK, 128), BF16), in...]
where the time goes in v5:
time: 30.6 us; the launch traced here: 30.5 us
  Pallas kernels  30.5 us (100%)
    pallas_call x1, Pallas kernels, body(): pl.pallas_call(kernel, out_shape=pltpu.VMEM((CHIPS, PACK, 128), BF16), in...  29.9 us
    pallas_call x1, Pallas kernels, body(): pl.pallas_call(finish, out_shape=jax.ShapeDtypeStruct((1, OUT, CORE), F32...  0.64 us

profile of v5, /device:TPU:1, one launch (start us, length us, event | category | flops | bytes accessed | tf_op | source)
XLA Modules:
  0.0 30.5 jit_solution(1446832224432913291)
XLA Ops:
  0.0 29.9 %shard_map.145.parts = bf16[8,80,128]{2,1,0:T(8,128)(2,1)S(1)} custom-call(s32[2,4]{1,0:T(2,128)} %foot_h.1, s32[2,2]{1,0:T(2,128)} %anchor_h.1, s32[2]{0:T(128)} %degree_h.1, s32[2,2,10]{2,1,0:T(2,128)} %bitcast.3, f32[2]{0:T(128)} %flux_h.1, f32[2]{0:T(128)} %variance_h.1, f32[10,2,1024]{2,1,0:T(2,128)} %bitcast.2, ...), custom_call_target="tpu_custom_call" | custom-call | tf_op jit(solution)/shard_map/pallas_call | solution.py:502
  29.9 0.6 %shard_map.146 = f32[1,24,384]{2,1,0:T(8,128)} custom-call(bf16[8,80,128]{2,1,0:T(8,128)(2,1)S(1)} %shard_map.145.parts), custom_call_target="tpu_custom_call" | custom-call | tf_op jit(solution)/shard_map/pallas_call | solution.py:569

commit v6 on v5

--- a/solution.py
+++ b/solution.py
@@ -444,7 +444,7 @@
     for chunk in range(2):
         cols = slice(SIDE * chunk, SIDE * chunk + SIDE)
         sums = num_own[:, pl.ds(start, BLK), cols]
-        for k, copy in zip(FAR, num_copies[len(FAR) * chunk :]):
+        for k, copy in list(zip(FAR, num_copies[len(FAR) * chunk :]))[::-1]:
             copy.wait_recv()
             sums = sums + num_in[chunk, k].astype(F32)
         s_re, s_im = (jnp.concatenate([sums[i], ex_sum[i, :, cols]], axis=0) * norm[:, cols] for i in range(2))
@@ -461,31 +461,35 @@
     image = dot(xtab[0], t_own[...])
     t_pair.wait_recv()
     image = image + dot(xtab[1], t_sib[...])
-    for t in range(CHIPS):
-        block = image[OUT * t : OUT * (t + 1)]
-        part_out[t] = jnp.concatenate(
-            [block[:, 128 * i : 128 * i + 128] for i in range(3)] + [jnp.zeros((PACK - 3 * OUT, 128), F32)], axis=0
-        ).astype(BF16)
+
     def part_copy(k):
         return describe(
             part_out.at[(z + k) % CHIPS], out.at[k], part_send.at[k], part_recv.at[k], {"exp": along(k)}
         )
 
-    to_others(PART_ORDER, part_copy)
+    for t in PART_ORDER:
+        block = image[OUT * t : OUT * (t + 1)]
+        part_out[t] = jnp.concatenate(
+            [block[:, LANES * i : LANES * (i + 1)] for i in range(3)] + [jnp.zeros((PACK - 3 * OUT, LANES), F32)], axis=0
+        ).astype(BF16)
+        to_others((t,), part_copy)
     parts = [part_copy(k) for k in FAR]
     mine = pltpu.make_async_copy(part_out.at[z], out.at[0], load_sem.at[0])
     mine.start()
     mine.wait()
-    for copy in parts:
-        copy.wait_recv()
     for i, copy in halos:
         pl.when(inside[i])(copy.wait_send)
-    for copy in psf_copies + num_pairs + [psf_pair, t_pair] + num_copies + parts:
+    for copy in psf_copies + num_pairs + [psf_pair, t_pair] + num_copies:
         copy.wait_send()
 
     @pl.when((p == 1) & (z < CHIPS - 1))
     def _():
         extra(z).wait_send()
+
+    for copy in parts:
+        copy.wait_recv()
+    for copy in parts:
+        copy.wait_send()
 
 
 def finish(parts, out):

time: 30.6 us -> 30.5 us (level)
  no operation moved by 1% of the time
where the time goes in v6:
time: 30.5 us; the launch traced here: 30.4 us
  Pallas kernels  30.4 us (100%)
    pallas_call x1, Pallas kernels, body(): pl.pallas_call(kernel, out_shape=pltpu.VMEM((CHIPS, PACK, 128), BF16), in...  29.8 us
    pallas_call x1, Pallas kernels, body(): pl.pallas_call(finish, out_shape=jax.ShapeDtypeStruct((1, OUT, CORE), F32...  0.64 us

profile of v6, /device:TPU:1, one launch (start us, length us, event | category | flops | bytes accessed | tf_op | source)
XLA Modules:
  0.0 30.4 jit_solution(564037751815122696)
XLA Ops:
  0.0 29.8 %shard_map.145.parts = bf16[8,80,128]{2,1,0:T(8,128)(2,1)S(1)} custom-call(s32[2,4]{1,0:T(2,128)} %foot_h.1, s32[2,2]{1,0:T(2,128)} %anchor_h.1, s32[2]{0:T(128)} %degree_h.1, s32[2,2,10]{2,1,0:T(2,128)} %bitcast.3, f32[2]{0:T(128)} %flux_h.1, f32[2]{0:T(128)} %variance_h.1, f32[10,2,1024]{2,1,0:T(2,128)} %bitcast.2, ...), custom_call_target="tpu_custom_call" | custom-call | tf_op jit(solution)/shard_map/pallas_call | solution.py:506
  29.8 0.6 %shard_map.146 = f32[1,24,384]{2,1,0:T(8,128)} custom-call(bf16[8,80,128]{2,1,0:T(8,128)(2,1)S(1)} %shard_map.145.parts), custom_call_target="tpu_custom_call" | custom-call | tf_op jit(solution)/shard_map/pallas_call | solution.py:573

commit v7 on v6

--- a/solution.py
+++ b/solution.py
@@ -19,7 +19,7 @@
 SIDE = TILE // 2
 LANES = 128
 FAR = (4, 3, 5, 2, 6, 1, 7)
-NUM_ORDER = (3, 2, 1, 4, 0, 5, 6, 7)
+NUM_ORDER = (2, 1, 3, 4, 0, 5, 6, 7)
 PART_ORDER = (0, 1, 2, 3, 4, 5, 6, 7)
 BLK = 16
 HALF = CHIPS * BLK

time: 30.5 us -> 30.8 us (level)
  no operation moved by 1% of the time
where the time goes in v7:
time: 30.8 us; the launch traced here: 30.7 us
  Pallas kernels  30.7 us (100%)
    pallas_call x1, Pallas kernels, body(): pl.pallas_call(kernel, out_shape=pltpu.VMEM((CHIPS, PACK, 128), BF16), in...  30.1 us
    pallas_call x1, Pallas kernels, body(): pl.pallas_call(finish, out_shape=jax.ShapeDtypeStruct((1, OUT, CORE), F32...  0.64 us

profile of v7, /device:TPU:1, one launch (start us, length us, event | category | flops | bytes accessed | tf_op | source)
XLA Modules:
  0.0 30.7 jit_solution(8118407887930250541)
XLA Ops:
  0.0 30.1 %shard_map.145.parts = bf16[8,80,128]{2,1,0:T(8,128)(2,1)S(1)} custom-call(s32[2,4]{1,0:T(2,128)} %foot_h.1, s32[2,2]{1,0:T(2,128)} %anchor_h.1, s32[2]{0:T(128)} %degree_h.1, s32[2,2,10]{2,1,0:T(2,128)} %bitcast.3, f32[2]{0:T(128)} %flux_h.1, f32[2]{0:T(128)} %variance_h.1, f32[10,2,1024]{2,1,0:T(2,128)} %bitcast.2, ...), custom_call_target="tpu_custom_call" | custom-call | tf_op jit(solution)/shard_map/pallas_call | solution.py:506
  30.1 0.6 %shard_map.146 = f32[1,24,384]{2,1,0:T(8,128)} custom-call(bf16[8,80,128]{2,1,0:T(8,128)(2,1)S(1)} %shard_map.145.parts), custom_call_target="tpu_custom_call" | custom-call | tf_op jit(solution)/shard_map/pallas_call | solution.py:573
